TPU v7x, 128 devices: a whole 4x4x4 slice. The times are simulated.
128 devices in a mesh: ctx: 64 (over y, z, x_lo, core), fsdp: 2 (over x_hi).
Axes of the slice: x: 4 (x_hi: 2, x_lo: 2; x = x_hi * 2 + x_lo), y: 4, z: 4, core: 2. Of those that a mesh axis runs over, the one named last changes fastest.
Arguments:
- hidden_in: bfloat16 [2, 8192, 1024], P('fsdp', 'ctx'), may hold values from -6 to 6
- doc_ids: int32 [2, 8192], P('fsdp'), may hold values from 0 to 2, as said below
- block_map: int32 [64], replicated, may hold values from 0 to 63, each once
- attn_gain: bfloat16 [1024], P('fsdp'), may hold values from 0.5 to 1.5
- attn_shift: bfloat16 [1024], P('fsdp'), may hold values from -1.5 to 1.5
- mlp_gain: bfloat16 [1024], P('fsdp'), may hold values from 0.5 to 1.5
- mlp_shift: bfloat16 [1024], P('fsdp'), may hold values from -1.5 to 1.5
- qkv_weight: bfloat16 [1024, 3072], P('fsdp'), may hold values from -0.1875 to 0.1875
- qkv_bias: bfloat16 [3072], P('fsdp'), may hold values from -1.5 to 1.5
- out_weight: bfloat16 [1024, 1024], P('fsdp'), may hold values from -1.5 to 1.5
- out_bias: bfloat16 [1024], P('fsdp'), may hold values from -1.5 to 1.5
- in_weight: bfloat16 [1024, 4096], P('fsdp'), may hold values from -0.1875 to 0.1875
- in_bias: bfloat16 [4096], P('fsdp'), may hold values from -1.5 to 1.5
- proj_weight: bfloat16 [4096, 1024], P('fsdp'), may hold values from -0.09375 to 0.09375
- proj_bias: bfloat16 [1024], P('fsdp'), may hold values from -1.5 to 1.5
- cotangent: bfloat16 [2, 8192, 1024], P('fsdp', 'ctx'), may hold values from -6 to 6
Outputs:
- hidden_out: bfloat16 [2, 8192, 1024], P('fsdp', 'ctx')
- hidden_grad: float32 [2, 8192, 1024], P('fsdp', 'ctx')
- attn_gain_grad: float32 [1024], P('fsdp')
- attn_shift_grad: float32 [1024], P('fsdp')
- mlp_gain_grad: float32 [1024], P('fsdp')
- mlp_shift_grad: float32 [1024], P('fsdp')
- qkv_weight_grad: float32 [1024, 3072], P('fsdp')
- qkv_bias_grad: float32 [3072], P('fsdp')
- out_weight_grad: float32 [1024, 1024], P('fsdp')
- out_bias_grad: float32 [1024], P('fsdp')
- in_weight_grad: float32 [1024, 4096], P('fsdp')
- in_bias_grad: float32 [4096], P('fsdp')
- proj_weight_grad: float32 [4096, 1024], P('fsdp')
- proj_bias_grad: float32 [1024], P('fsdp')
Inputs may be any that keep to these rules, and one draw needn't show every extreme that they name: `doc_ids`: each row is nondecreasing along the stream, holds every document number, and document 0 covers at least the first half of the stream. `block_map`: a permutation of the block pairs.
All inputs are finite; a program needn't handle non-finite values.
Results may differ from a plain program's by a relative error of at most 0.012.
Values may be sent and summed in bfloat16 or wider, within the bound.
No kernel may reach another device: no remote copies, remote signals or barrier semaphores. Data moves between devices by JAX's collectives and lax.ppermute only.
A program may use at most 320 MiB of HBM per device.

v0:
```python
import math

import jax
import jax.numpy as jnp
from jax import lax
from jax.sharding import PartitionSpec as P

HEADS = 16
HEAD_DIM = 64
ROT = 16
DOCS = 3


EPS = 1e-05
NEG_FILL = -1e30


def norm_apply(hidden, gain, shift):
    centre = jnp.mean(hidden, axis=-1, keepdims=True)
    moved = hidden - centre
    spread = jnp.mean(moved * moved, axis=-1, keepdims=True)
    return moved * lax.rsqrt(spread + EPS) * gain + shift


def frequencies():
    return 10000.0 ** (-(jnp.arange(0, ROT, 2).astype(jnp.float32) / ROT))


def rotate(heads_in, angles):
    cosine = jnp.cos(angles)
    sine = jnp.sin(angles)
    cosine = jnp.concatenate([cosine, cosine], axis=-1)[..., None, :]
    sine = jnp.concatenate([sine, sine], axis=-1)[..., None, :]
    turned_part = heads_in[..., :ROT]
    first_half = turned_part[..., : ROT // 2]
    second_half = turned_part[..., ROT // 2 :]
    turned = turned_part * cosine + jnp.concatenate([-second_half, first_half], axis=-1) * sine
    return jnp.concatenate([turned, heads_in[..., ROT:]], axis=-1)


def stream_positions(block_map, half_rows):
    pair_count = block_map.shape[0]
    offsets = jnp.arange(half_rows, dtype=jnp.int32)
    lower_rows = block_map[:, None] * half_rows + offsets[None, :]
    upper_rows = (2 * pair_count - 1 - block_map)[:, None] * half_rows + offsets[None, :]
    return jnp.concatenate([lower_rows, upper_rows], axis=1)


def split_blocks(block_width, array_in):
    return array_in.reshape((array_in.shape[0] // block_width, block_width) + array_in.shape[1:])


def masked_scores(queries, key_block, query_pos, query_doc, key_pos, key_doc):
    scores = jnp.einsum(
        "qhd,khd->hqk", queries, key_block, preferred_element_type=jnp.float32
    ) * HEAD_DIM ** (-0.5)
    allowed = (key_pos[None, :] <= query_pos[:, None]) & (key_doc[None, :] == query_doc[:, None])
    return jnp.where(allowed[None], scores, NEG_FILL)


def attend_forward(queries, keys, values, query_pos, query_doc, key_pos, key_doc):
    block_width = math.gcd(keys.shape[0], 1024)
    stacked = (
        split_blocks(block_width, keys),
        split_blocks(block_width, values),
        split_blocks(block_width, key_pos),
        split_blocks(block_width, key_doc),
    )
    heads_rows = (queries.shape[1], queries.shape[0])

    def scan_top(state_now, key_block):
        running, exp_total = state_now
        scores = masked_scores(
            queries, key_block[0], query_pos, query_doc, key_block[2], key_block[3]
        )
        new_top = jnp.maximum(running, jnp.max(scores, axis=-1))
        exp_total = exp_total * jnp.exp(running - new_top) + jnp.sum(
            jnp.exp(scores - new_top[..., None]), axis=-1
        )
        return ((new_top, exp_total), None)

    initial = (jnp.full(heads_rows, NEG_FILL, jnp.float32), jnp.zeros(heads_rows, jnp.float32))
    (running, exp_total), _ = lax.scan(scan_top, initial, stacked)
    log_total = running + jnp.log(exp_total)

    def scan_values(state_now, key_block):
        scores = masked_scores(
            queries, key_block[0], query_pos, query_doc, key_block[2], key_block[3]
        )
        chances = jnp.exp(scores - log_total[..., None]).astype(jnp.bfloat16)
        return (
            state_now
            + jnp.einsum("hqk,khd->qhd", chances, key_block[1], preferred_element_type=jnp.float32),
            None,
        )

    mixed_sum, _ = lax.scan(scan_values, jnp.zeros(queries.shape, jnp.float32), stacked)
    return (mixed_sum, log_total)


def block_grads(queries, mixed_grad, log_total, row_delta, query_pos, query_doc, key_block):
    keys, values, key_pos, key_doc = key_block
    scale = HEAD_DIM ** (-0.5)
    scores = masked_scores(queries, keys, query_pos, query_doc, key_pos, key_doc)
    chances = jnp.exp(scores - log_total[..., None])
    along_value = jnp.einsum("qhd,khd->hqk", mixed_grad, values, preferred_element_type=jnp.float32)
    score_grad = (chances * (along_value - row_delta[..., None])).astype(jnp.bfloat16)
    query_grad = None
    key_terms_out = None
    query_grad = (
        jnp.einsum("hqk,khd->qhd", score_grad, keys, preferred_element_type=jnp.float32) * scale
    )
    key_grad = (
        jnp.einsum("hqk,qhd->khd", score_grad, queries, preferred_element_type=jnp.float32) * scale
    )
    value_grad = jnp.einsum(
        "hqk,qhd->khd", chances.astype(jnp.bfloat16), mixed_grad, preferred_element_type=jnp.float32
    )
    key_rows = keys.shape[0]
    key_terms_out = jnp.concatenate(
        [key_grad.reshape(key_rows, -1), value_grad.reshape(key_rows, -1)], axis=1
    )
    return (query_grad, key_terms_out)


def attend_back(
    queries, mixed_grad, log_total, row_delta, query_pos, query_doc, keys, values, key_pos, key_doc
):
    block_width = math.gcd(keys.shape[0], 1024)
    stacked = (
        split_blocks(block_width, keys),
        split_blocks(block_width, values),
        split_blocks(block_width, key_pos),
        split_blocks(block_width, key_doc),
    )

    def scan_back(state_now, key_block):
        query_grad, key_terms_out = block_grads(
            queries, mixed_grad, log_total, row_delta, query_pos, query_doc, key_block
        )
        state_now = state_now + query_grad
        return (state_now, key_terms_out)

    total_grad, grad_terms = lax.scan(scan_back, jnp.zeros(queries.shape, jnp.float32), stacked)
    grad_terms = grad_terms.reshape(keys.shape[0], -1)
    return (total_grad, grad_terms)


def per_device(
    hidden_in,
    doc_ids,
    block_map,
    attn_gain,
    attn_shift,
    mlp_gain,
    mlp_shift,
    qkv_weight,
    qkv_bias,
    out_weight,
    out_bias,
    in_weight,
    in_bias,
    proj_weight,
    proj_bias,
    cotangent,
):
    gathered = (
        lax.all_gather(attn_gain, "fsdp", axis=0, tiled=True),
        lax.all_gather(attn_shift, "fsdp", axis=0, tiled=True),
        lax.all_gather(mlp_gain, "fsdp", axis=0, tiled=True),
        lax.all_gather(mlp_shift, "fsdp", axis=0, tiled=True),
        lax.all_gather(qkv_weight, "fsdp", axis=0, tiled=True),
        lax.all_gather(qkv_bias, "fsdp", axis=0, tiled=True),
        lax.all_gather(out_weight, "fsdp", axis=0, tiled=True),
        lax.all_gather(out_bias, "fsdp", axis=0, tiled=True),
        lax.all_gather(in_weight, "fsdp", axis=0, tiled=True),
        lax.all_gather(in_bias, "fsdp", axis=0, tiled=True),
        lax.all_gather(proj_weight, "fsdp", axis=0, tiled=True),
        lax.all_gather(proj_bias, "fsdp", axis=0, tiled=True),
    )
    attn_gain_all = gathered[0].astype(jnp.float32)
    attn_shift_all = gathered[1].astype(jnp.float32)
    mlp_gain_all = gathered[2].astype(jnp.float32)
    mlp_shift_all = gathered[3].astype(jnp.float32)
    qkv_all = gathered[4]
    qkv_bias_all = gathered[5].astype(jnp.float32)
    out_all = gathered[6]
    out_bias_all = gathered[7].astype(jnp.float32)
    in_all = gathered[8]
    in_bias_all = gathered[9].astype(jnp.float32)
    proj_all = gathered[10]
    proj_bias_all = gathered[11].astype(jnp.float32)
    row_count = hidden_in.shape[1]
    width_all = HEADS * HEAD_DIM
    device_place = lax.axis_index("ctx")
    layout = stream_positions(block_map, row_count // 2)
    key_pos = layout.reshape(-1)
    query_pos = lax.dynamic_index_in_dim(layout, device_place, 0, keepdims=False)
    segment = doc_ids[0]
    key_doc = jnp.take(segment, key_pos)
    query_doc = jnp.take(segment, query_pos)
    labels = jnp.arange(DOCS, dtype=jnp.int32)
    starts = jnp.sum((segment[None, :] < labels[:, None]).astype(jnp.int32), axis=1)
    doc_first = jnp.sum(
        jnp.where(query_doc[:, None] == labels[None, :], starts[None, :], 0), axis=1
    )
    angles = (query_pos - doc_first).astype(jnp.float32)[:, None] * frequencies()[None, :]
    hidden = hidden_in[0].astype(jnp.float32)
    normed = norm_apply(hidden, attn_gain_all, attn_shift_all).astype(jnp.bfloat16)
    project = jnp.dot(normed, qkv_all, preferred_element_type=jnp.float32) + qkv_bias_all
    shaped = project.reshape(row_count, 3, HEADS, HEAD_DIM)
    query_lin = shaped[:, 0]
    key_lin = shaped[:, 1]
    queries = rotate(query_lin, angles).astype(jnp.bfloat16)
    keys_here = rotate(key_lin, angles).astype(jnp.bfloat16)
    values_here = shaped[:, 2].astype(jnp.bfloat16)
    keys_all, values_all = (
        lax.all_gather(keys_here.reshape(row_count, width_all), "ctx", axis=0, tiled=True),
        lax.all_gather(values_here.reshape(row_count, width_all), "ctx", axis=0, tiled=True),
    )
    total_rows = keys_all.shape[0]
    keys_all = keys_all.reshape(total_rows, HEADS, HEAD_DIM)
    values_all = values_all.reshape(total_rows, HEADS, HEAD_DIM)
    mixed_sum, log_total = attend_forward(
        queries, keys_all, values_all, query_pos, query_doc, key_pos, key_doc
    )
    mixed_low = mixed_sum.reshape(row_count, width_all).astype(jnp.bfloat16)
    branch_attn = jnp.dot(mixed_low, out_all, preferred_element_type=jnp.float32) + out_bias_all
    normed_mlp = norm_apply(hidden, mlp_gain_all, mlp_shift_all).astype(jnp.bfloat16)
    inner_act = jnp.dot(normed_mlp, in_all, preferred_element_type=jnp.float32) + in_bias_all
    active = jax.nn.gelu(inner_act, approximate=False).astype(jnp.bfloat16)
    branch_mlp = jnp.dot(active, proj_all, preferred_element_type=jnp.float32) + proj_bias_all
    hidden_out = (hidden + branch_attn + branch_mlp).astype(jnp.bfloat16)[None]
    upstream = cotangent[0]
    upstream_full = upstream.astype(jnp.float32)
    proj_weight_grad = jnp.dot(active.T, upstream, preferred_element_type=jnp.float32)
    proj_bias_grad = jnp.sum(upstream_full, axis=0)
    out_weight_grad = jnp.dot(mixed_low.T, upstream, preferred_element_type=jnp.float32)
    mixed_grad = (
        jnp.dot(upstream, out_all.T, preferred_element_type=jnp.float32)
        .astype(jnp.bfloat16)
        .reshape(row_count, HEADS, HEAD_DIM)
    )
    row_delta = jnp.einsum("qhd,qhd->hq", mixed_grad.astype(jnp.float32), mixed_sum)
    query_grad, grad_terms = attend_back(
        queries,
        mixed_grad,
        log_total,
        row_delta,
        query_pos,
        query_doc,
        keys_all,
        values_all,
        key_pos,
        key_doc,
    )
    key_value_grad = lax.psum_scatter(grad_terms, "ctx", scatter_dimension=0, tiled=True)
    key_rot_grad = key_value_grad[:, :width_all].reshape(row_count, HEADS, HEAD_DIM)
    value_grad = key_value_grad[:, width_all:]
    _, turn_back = jax.vjp(lambda moved: rotate(moved, angles), query_lin)
    (query_lin_grad,) = turn_back(query_grad)
    (key_lin_grad,) = turn_back(key_rot_grad)
    project_grad = jnp.concatenate(
        [
            query_lin_grad.reshape(row_count, width_all),
            key_lin_grad.reshape(row_count, width_all),
            value_grad,
        ],
        axis=1,
    ).astype(jnp.bfloat16)
    qkv_weight_grad = jnp.dot(normed.T, project_grad, preferred_element_type=jnp.float32)
    qkv_bias_grad = jnp.sum(project_grad.astype(jnp.float32), axis=0)
    normed_grad = jnp.dot(project_grad, qkv_all.T, preferred_element_type=jnp.float32)
    active_grad = jnp.dot(upstream, proj_all.T, preferred_element_type=jnp.float32)
    _, gelu_back = jax.vjp(lambda inside: jax.nn.gelu(inside, approximate=False), inner_act)
    inner_grad = gelu_back(active_grad)[0].astype(jnp.bfloat16)
    in_weight_grad = jnp.dot(normed_mlp.T, inner_grad, preferred_element_type=jnp.float32)
    in_bias_grad = jnp.sum(inner_grad.astype(jnp.float32), axis=0)
    normed_mlp_grad = jnp.dot(inner_grad, in_all.T, preferred_element_type=jnp.float32)
    _, attn_norm_back = jax.vjp(norm_apply, hidden, attn_gain_all, attn_shift_all)
    attn_input_grad, attn_gain_grad, attn_shift_grad = attn_norm_back(normed_grad)
    _, mlp_norm_back = jax.vjp(norm_apply, hidden, mlp_gain_all, mlp_shift_all)
    mlp_input_grad, mlp_gain_grad, mlp_shift_grad = mlp_norm_back(normed_mlp_grad)
    hidden_grad = (upstream_full + attn_input_grad + mlp_input_grad)[None]
    summed = (
        lax.psum_scatter(
            attn_gain_grad.astype(jnp.bfloat16), "fsdp", scatter_dimension=0, tiled=True
        ).astype(jnp.float32),
        lax.psum_scatter(
            attn_shift_grad.astype(jnp.bfloat16), "fsdp", scatter_dimension=0, tiled=True
        ).astype(jnp.float32),
        lax.psum_scatter(
            mlp_gain_grad.astype(jnp.bfloat16), "fsdp", scatter_dimension=0, tiled=True
        ).astype(jnp.float32),
        lax.psum_scatter(
            mlp_shift_grad.astype(jnp.bfloat16), "fsdp", scatter_dimension=0, tiled=True
        ).astype(jnp.float32),
        lax.psum_scatter(
            qkv_weight_grad.astype(jnp.bfloat16), "fsdp", scatter_dimension=0, tiled=True
        ).astype(jnp.float32),
        lax.psum_scatter(
            qkv_bias_grad.astype(jnp.bfloat16), "fsdp", scatter_dimension=0, tiled=True
        ).astype(jnp.float32),
        lax.psum_scatter(
            out_weight_grad.astype(jnp.bfloat16), "fsdp", scatter_dimension=0, tiled=True
        ).astype(jnp.float32),
        lax.psum_scatter(
            proj_bias_grad.astype(jnp.bfloat16), "fsdp", scatter_dimension=0, tiled=True
        ).astype(jnp.float32),
        lax.psum_scatter(
            in_weight_grad.astype(jnp.bfloat16), "fsdp", scatter_dimension=0, tiled=True
        ).astype(jnp.float32),
        lax.psum_scatter(
            in_bias_grad.astype(jnp.bfloat16), "fsdp", scatter_dimension=0, tiled=True
        ).astype(jnp.float32),
        lax.psum_scatter(
            proj_weight_grad.astype(jnp.bfloat16), "fsdp", scatter_dimension=0, tiled=True
        ).astype(jnp.float32),
        lax.psum_scatter(
            proj_bias_grad.astype(jnp.bfloat16), "fsdp", scatter_dimension=0, tiled=True
        ).astype(jnp.float32),
    )
    totals = lax.psum(
        (
            summed[0],
            summed[1],
            summed[2],
            summed[3],
            summed[4],
            summed[5],
            summed[6],
            summed[7],
            summed[8],
            summed[9],
            summed[10],
            summed[11],
        ),
        "ctx",
    )
    return (
        hidden_out,
        hidden_grad,
        totals[0],
        totals[1],
        totals[2],
        totals[3],
        totals[4],
        totals[5],
        totals[6],
        totals[7],
        totals[8],
        totals[9],
        totals[10],
        totals[11],
    )


def solution(mesh):
    in_specs = (
        P("fsdp", "ctx", None),
        P("fsdp", None),
        P(),
        P("fsdp"),
        P("fsdp"),
        P("fsdp"),
        P("fsdp"),
        P("fsdp", None),
        P("fsdp"),
        P("fsdp", None),
        P("fsdp"),
        P("fsdp", None),
        P("fsdp"),
        P("fsdp", None),
        P("fsdp"),
        P("fsdp", "ctx", None),
    )
    out_specs = (
        P("fsdp", "ctx", None),
        P("fsdp", "ctx", None),
        P("fsdp"),
        P("fsdp"),
        P("fsdp"),
        P("fsdp"),
        P("fsdp", None),
        P("fsdp"),
        P("fsdp", None),
        P("fsdp"),
        P("fsdp", None),
        P("fsdp"),
        P("fsdp", None),
        P("fsdp"),
    )
    return jax.shard_map(
        per_device, mesh=mesh, in_specs=in_specs, out_specs=out_specs, check_vma=False
    )
```

profile of v0, /device:TPU:0, one launch (start us, length us, event | category | flops | bytes accessed | tf_op | source)
XLA Modules:
  0.0 2620.6 jit_solution(16965242461717531914)
XLA Ops:
  26.8 69.8 %all-gather.14.cloned.1.call-done = bf16[1024,3072]{1,0:T(8,128)(2,1)} async-done(((bf16[512,3072]{1,0:T(8,128)(2,1)}), bf16[1024,3072]{1,0:T(8,128)(2,1)}) %all-gather.14.cloned.1.call-update) | async-done | bytes 6291472 | tf_op jit(solution)/shard_map/all_gather | solution.py:172
  106.3 45.5 %gather_fusion = s32[8192]{0:T(1024)S(1)} fusion(s32[8192]{0:T(1024)S(1)} %bitcast.304, s32[8192]{0:T(1024)S(1)} %broadcast_clamp_fusion), kind=kCustom, calls=%fused_computation | custom fusion | bytes 98304 | tf_op jit(solution)/shard_map/jit(_take)/gather | solution.py:200
  155.6 142.1 %all-gather.16.cloned.1.call-done = bf16[8192,1024]{0,1:T(8,128)(2,1)} async-done(((bf16[128,1024]{0,1:T(8,128)(2,1)}), bf16[8192,1024]{0,1:T(8,128)(2,1)}) %all-gather.16.cloned.1.call-update) | async-done | bytes 16777232 | tf_op jit(solution)/shard_map/all_gather | solution.py:219
  297.7 15.6 copy.116
  313.3 20.6 copy.74
  333.9 128.4 %all-gather.18.cloned.1.call-done = bf16[8192,1024]{0,1:T(8,128)(2,1)} async-done(((bf16[128,1024]{0,1:T(8,128)(2,1)}), bf16[8192,1024]{0,1:T(8,128)(2,1)}) %all-gather.18.cloned.1.call-update) | async-done | bytes 16777232 | tf_op jit(solution)/shard_map/all_gather | solution.py:218
  462.3 15.6 copy.117
  478.0 20.7 copy.75
  498.6 100.1 %while.37 = (s32[]{:T(128)}, f32[16,128]{1,0:T(8,128)S(1)}, f32[16,128]{1,0:T(8,128)S(1)}, s32[8,1024]{1,0:T(8,128)S(1)}, s32[128]{0:T(128)S(1)}, /*index=5*/s32...) while((s32[]{:T(128)}, f32[16,128]{1,0:T(8,128)S(1)}, ...), condition=%wide.region_7.8_spmd.clone, body=%wide.region_4.7_spmd.clone.sunk | while | flops 283518976 | bytes 19661960 | solution.py:83
  536.0 6.8 fusion.173
  572.8 6.8 fusion.173
  585.1 7.8 fusion.173
  598.7 45.8 %while.38 = (s32[]{:T(128)}, f32[128,16,64]{0,2,1:T(8,128)S(1)}, bf16[8,1024,16,64]{1,3,2,0:T(8,128)(2,1)}, s32[8,1024]{1,0:T(8,128)S(1)}, s32[128]{0:T(128)S(1)...) while((s32[]{:T(128)}, f32[128,16,64]{0,2,1:T(8,128)S(1)}, ...), condition=%wide.region_9.10_spmd.clone, body=%wide.region_8.9_spmd.clone.sunk | while | flops 545914880 | bytes 5802634 | solution.py:97
  645.3 352.1 %while.39 = (s32[]{:T(128)}, f32[128,16,64]{0,2,1:T(8,128)S(1)}, f32[8,1024,2048]{2,1,0:T(8,128)}, bf16[8,1024,16,64]{1,3,2,0:T(8,128)(2,1)}, s32[8,1024]{1,0:T(...) while((s32[]{:T(128)}, f32[128,16,64]{0,2,1:T(8,128)S(1)}, ...), condition=%wide.region_11.12_spmd.clone, body=%wide.region_10.11_spmd.clone.sunk | while | flops 1367080960 | bytes 155632880 | solution.py:144
  649.1 8.3 fusion.191
  672.8 9.1 copy.119
  682.0 7.8 constant_dynamic-update-slice_fusion.2
  693.1 8.3 fusion.191
  716.8 9.1 copy.119
  726.0 7.7 constant_dynamic-update-slice_fusion.2
  737.0 8.3 fusion.191
  760.8 9.1 copy.119
  769.9 7.8 constant_dynamic-update-slice_fusion.2
  781.0 8.3 fusion.191
  804.8 9.1 copy.119
  813.9 7.7 constant_dynamic-update-slice_fusion.2
  825.0 8.3 fusion.191
  848.7 9.1 copy.119
  857.9 7.7 constant_dynamic-update-slice_fusion.2
  868.9 8.3 fusion.191
  892.7 9.1 copy.119
  901.8 7.7 constant_dynamic-update-slice_fusion.2
  912.9 8.3 fusion.191
  936.7 9.1 copy.119
  945.8 7.7 constant_dynamic-update-slice_fusion.2
  956.9 8.3 fusion.191
  980.6 9.1 copy.119
  989.8 7.7 constant_dynamic-update-slice_fusion.2
  998.2 9.0 all_gather.53
  1018.9 9.3 multiply_convert_fusion
  1028.3 10.4 fusion.126
  1055.4 670.1 %reduce-scatter.6.cloned.1.call-done = f32[128,2048]{1,0:T(8,128)} async-done(((f32[8192,2048]{1,0:T(8,128)}), f32[128,2048]{1,0:T(8,128)}) %reduce-scatter.6.cloned.1.call-update) | async-done | bytes 1048592 | tf_op jit(solution)/shard_map/reduce_scatter | solution.py:257
  1768.6 59.7 %reduce-scatter.12.cloned.1.call-done = bf16[512,4096]{1,0:T(8,128)(2,1)} async-done(((bf16[1024,4096]{1,0:T(8,128)(2,1)}), bf16[512,4096]{1,0:T(8,128)(2,1)}) %reduce-scatter.12.cloned.1.call-update) | async-done | bytes 4194320 | tf_op jit(solution)/shard_map/reduce_scatter | solution.py:310
  1828.3 105.9 %reduce-scatter.14.cloned.1.call-done = bf16[2048,1024]{1,0:T(8,128)(2,1)} async-done(((bf16[4096,1024]{1,0:T(8,128)(2,1)}), bf16[2048,1024]{1,0:T(8,128)(2,1)}) %reduce-scatter.14.cloned.1.call-update) | async-done | bytes 4194320 | tf_op jit(solution)/shard_map/reduce_scatter | solution.py:316
  1937.1 35.2 %reduce-scatter.10.cloned.1.call-done = bf16[512,1024]{1,0:T(8,128)(2,1)} async-done(((bf16[1024,1024]{1,0:T(8,128)(2,1)}), bf16[512,1024]{1,0:T(8,128)(2,1)}) %reduce-scatter.10.cloned.1.call-update) | async-done | bytes 1048592 | tf_op jit(solution)/shard_map/reduce_scatter | solution.py:304
  1978.2 8.6 all-reduce.16
  1988.4 67.6 %reduce-scatter.8.cloned.1.call-done = bf16[512,3072]{1,0:T(8,128)(2,1)} async-done(((bf16[1024,3072]{1,0:T(8,128)(2,1)}), bf16[512,3072]{1,0:T(8,128)(2,1)}) %reduce-scatter.8.cloned.1.call-update) | async-done | bytes 3145744 | tf_op jit(solution)/shard_map/reduce_scatter | solution.py:298
  2056.0 557.3 %all-reduce.18 = (f32[512]{0:T(512)}, f32[512]{0:T(512)}, f32[512]{0:T(512)}, f32[512]{0:T(512)}, f32[512,3072]{1,0:T(8,128)}, /*index=5*/f32[1536]{0:T(1024)}, ...) all-reduce(f32[512]{0:T(512)S(1)} %dynamic-slice_convert_fusion.6, ...), channel_id=1, replica_groups=mesh['ctx'=64,'fsdp'=2] {'ctx'}, use_global_device_ids=true, to_apply=%region_19.20 | all-reduce | flops 6297600 | bytes 37797888 | tf_op jit(solution)/shard_map/psum | solution.py:323
  (375 shorter events, 387.8 us)
Async XLA Ops:
  7.2 7.5 copy-start.35
  7.2 13.3 copy-start.36
  7.2 19.2 copy-start.3
  7.2 89.4 %all-gather.14.cloned.1.call-start = ((), (), s32[]{:S(2)}) async-start(), calls=%async_computation.5 | async-start | bytes 9437184 | tf_op jit(solution)/shard_map/all_gather | solution.py:172
  8.0 143.9 %all-gather.20.cloned.1.call-start = ((), (), s32[]{:S(2)}) async-start(), calls=%async_computation.8 | async-start | bytes 3145728 | tf_op jit(solution)/shard_map/all_gather | solution.py:174
  8.7 289.0 %all-gather.16.cloned.1.call-start = ((), (), s32[]{:S(2)}) async-start(), calls=%async_computation.6 | async-start | bytes 17039360 | tf_op jit(solution)/shard_map/all_gather | solution.py:219
  20.5 76.1 %copy-start.18 = (f32[2,1,512]{2,1,0:T(1,128)}, f32[2,1,512]{2,1,0:T(1,128)S(1)}, u32[]{:S(2)}) copy-start(f32[2,1,512]{2,1,0:T(1,128)S(1)} %convert_element_type.205) | copy-start | bytes 12292
  26.4 70.2 %copy-start.16 = (f32[2,1,512]{2,1,0:T(1,128)}, f32[2,1,512]{2,1,0:T(1,128)S(1)}, u32[]{:S(2)}) copy-start(f32[2,1,512]{2,1,0:T(1,128)S(1)} %convert_element_type.204) | copy-start | bytes 12292
  26.6 70.1 %copy-start.23 = (f32[128]{0:T(128)}, f32[128]{0:T(128)S(1)}, u32[]{:S(2)}) copy-start(f32[128]{0:T(128)S(1)} %broadcast_multiply_fusion.1) | copy-start | bytes 1540
  26.8 69.8 %copy-start.32 = (f32[128]{0:T(128)}, f32[128]{0:T(128)S(1)}, u32[]{:S(2)}) copy-start(f32[128]{0:T(128)S(1)} %fusion.97) | copy-start | bytes 1540
  26.8 69.8 %copy-start.25 = (f32[128]{0:T(128)}, f32[128]{0:T(128)S(1)}, u32[]{:S(2)}) copy-start(f32[128]{0:T(128)S(1)} %fusion.114) | copy-start | bytes 1540
  101.8 360.6 %all-gather.18.cloned.1.call-start = ((), (), s32[]{:S(2)}) async-start(), calls=%async_computation.7 | async-start | bytes 17039360 | tf_op jit(solution)/shard_map/all_gather | solution.py:218
  104.7 914.2 %all-gather.22.cloned.1.call-start = ((), (), s32[]{:S(2)}) async-start(), calls=%async_computation.9 | async-start | bytes 12582912 | tf_op jit(solution)/shard_map/all_gather | solution.py:176
  105.3 923.0 %all-gather.24.cloned.1.call-start = ((), (), s32[]{:S(2)}) async-start(), calls=%async_computation.10 | async-start | bytes 12582912 | tf_op jit(solution)/shard_map/all_gather | solution.py:178
  105.8 1619.7 %reduce-scatter.6.cloned.1.call-start = ((), (), s32[]{:S(2)}) async-start(), calls=%async_computation.11 | async-start | bytes 68157440 | tf_op jit(solution)/shard_map/reduce_scatter | solution.py:257
  106.2 45.6 %copy-start.5 = (bf16[1,128,1024]{2,1,0:T(8,128)(2,1)S(1)}, bf16[1,128,1024]{2,1,0:T(8,128)(2,1)}, u32[]{:S(2)}) copy-start(bf16[1,128,1024]{2,1,0:T(8,128)(2,1)} %param.37) | copy-start | bytes 786436
  648.7 8.7 copy-start.1
  661.2 5.9 copy-start.2
  692.7 8.7 copy-start.1
  705.2 5.9 copy-start.2
  736.6 8.7 copy-start.1
  749.1 5.9 copy-start.2
  780.6 8.7 copy-start.1
  793.1 5.9 copy-start.2
  824.6 8.7 copy-start.1
  868.6 8.7 copy-start.1
  881.0 5.9 copy-start.2
  912.5 8.7 copy-start.1
  925.0 5.9 copy-start.2
  956.5 8.7 copy-start.1
  997.5 9.6 copy-start.37
  997.5 15.5 copy-start.38
  997.5 21.4 copy-start.4
  997.5 21.4 copy-start.24
  997.5 21.4 copy-start.26
  997.5 830.8 %reduce-scatter.12.cloned.1.call-start = ((), (), s32[]{:S(2)}) async-start(), calls=%async_computation.14 | async-start | bytes 12582912 | tf_op jit(solution)/shard_map/reduce_scatter | solution.py:310
  1018.9 9.4 copy-start.6
  1044.6 889.6 %reduce-scatter.14.cloned.1.call-start = ((), (), s32[]{:S(2)}) async-start(), calls=%async_computation.15 | async-start | bytes 12582912 | tf_op jit(solution)/shard_map/reduce_scatter | solution.py:316
  1050.5 921.9 %reduce-scatter.10.cloned.1.call-start = ((), (), s32[]{:S(2)}) async-start(), calls=%async_computation.13 | async-start | bytes 3145728 | tf_op jit(solution)/shard_map/reduce_scatter | solution.py:304
  1054.3 676.2 %copy-start.22 = (f32[128,16]{0,1:T(8,128)S(1)}, f32[128,16]{0,1:T(8,128)}, u32[]{:S(2)}) copy-start(f32[128,16]{0,1:T(8,128)} %copy-done.21) | copy-start | bytes 24580
  1054.3 1001.7 %reduce-scatter.8.cloned.1.call-start = ((), (), s32[]{:S(2)}) async-start(), calls=%async_computation.12 | async-start | bytes 9437184 | tf_op jit(solution)/shard_map/reduce_scatter | solution.py:298
  1734.8 6.5 copy-start.7
  1741.3 6.5 copy-start.40
  1741.3 13.0 copy-start.42
  1763.1 171.1 %copy-start.12 = (bf16[128,16,64]{0,2,1:T(8,128)(2,1)S(1)}, bf16[128,16,64]{0,2,1:T(8,128)(2,1)}, u32[]{:S(2)}) copy-start(bf16[128,16,64]{0,2,1:T(8,128)(2,1)} %copy-done.11) | copy-start | bytes 786436
  1768.6 203.7 %copy-start.8 = (bf16[128,1024]{1,0:T(8,128)(2,1)S(1)}, bf16[128,1024]{1,0:T(8,128)(2,1)}, u32[]{:S(2)}) copy-start(bf16[128,1024]{1,0:T(8,128)(2,1)} %copy-done.7) | copy-start | bytes 786436
  1768.6 203.7 %copy-start.10 = (bf16[128,1024]{1,0:T(8,128)(2,1)S(1)}, bf16[128,1024]{1,0:T(8,128)(2,1)}, u32[]{:S(2)}) copy-start(bf16[128,1024]{1,0:T(8,128)(2,1)} %copy-done.9) | copy-start | bytes 786436
  1977.6 78.4 %copy-start.15 = (bf16[512,1024]{1,0:T(8,128)(2,1)S(1)}, bf16[512,1024]{1,0:T(8,128)(2,1)}, u32[]{:S(2)}) copy-start(bf16[512,1024]{1,0:T(8,128)(2,1)} %reduce-scatter.10.cloned.1.call-done) | copy-start | bytes 3145732
  (20 other events, 59.1 us)
Sparse Core Ops, SparseCore 0:
  9.7 86.8 all-gather.13
  98.3 36.5 all-gather.19
  137.1 160.5 all-gather.15
  299.7 162.5 all-gather.17
  463.8 111.9 all-gather.21
  577.3 107.4 all-gather.23
  997.7 727.8 reduce-scatter.5
  1728.5 99.7 reduce-scatter.11
  1831.5 102.7 reduce-scatter.13
  1937.0 35.2 reduce-scatter.9
  1975.4 80.5 reduce-scatter.7
where the time goes:
time: 2630 us; the launch traced here: 2620 us
  waiting for transfers between devices  1280 us (49%)
  blocking collectives  616 us (23%)
  matrix products  342 us (13%)
  local copies, waits for them, and re-layouts  268 us (10%)
  other arithmetic  93.4 us (4%)
    reduce_scatter x1, waiting for transfers between devices, per_device(): lax.psum_scatter(grad_terms, 'ctx', scatter_dimension=0, tiled=True)  670 us
    psum x1, blocking collectives, per_device(): lax.psum((summed[0], summed[1], summed[2], summed[3], summed[4], summed[5...  557 us
    all_gather x1, waiting for transfers between devices, per_device(): lax.all_gather(values_here.reshape(row_count, width_all), 'ctx', axis=0,...  142 us
    dynamic_update_slice x16, local copies, waits for them, and re-layouts, attend_back(): lax.scan(scan_back, jnp.zeros(queries.shape, jnp.float32), stacked)  135 us
    all_gather x1, waiting for transfers between devices, per_device(): lax.all_gather(keys_here.reshape(row_count, width_all), 'ctx', axis=0, ti...  128 us
    reduce_scatter x1, waiting for transfers between devices, per_device(): lax.psum_scatter(proj_weight_grad.astype(jnp.bfloat16), 'fsdp', scatter_d...  106 us
    dot_general x16, matrix products, masked_scores(): jnp.einsum('qhd,khd->hqk', queries, key_block, preferred_element_type=jnp...  78.9 us
    unnamed x95, local copies, waits for them, and re-layouts  76.5 us
  transfers between devices with their start and end apart: 11, of which 8 were waited for; matrix products, arithmetic and copies ran while one was open for 27% of the time, Pallas kernels for 0%

commit v1 on v0

v1 whole, which is shorter than its diff:
```python
import functools
import math

import jax
import jax.numpy as jnp
from jax import lax
from jax.experimental import pallas as pl
from jax.experimental.pallas import tpu as pltpu
from jax.sharding import Mesh
from jax.sharding import PartitionSpec as P

ROT = 16
EPS = 1e-05
NEG_FILL = -1e30
BF = jnp.bfloat16
F32 = jnp.float32
RING = ("xh", "xl")
PLANE = ("y", "z")
MIB = 1 << 20

NN = (((1,), (0,)), ((), ()))
NT = (((1,), (1,)), ((), ()))
TN = (((0,), (0,)), ((), ()))


def mm(left, right, dims=NN):
    return lax.dot_general(left, right, dims, preferred_element_type=F32)


def mult(value, step):
    return pl.multiple_of(value, step)


def whole(space=pltpu.VMEM):
    return pl.BlockSpec(memory_space=space)


def call(body, outs, ins, scratch=(), flops=0, moved=0, limit=48):
    return pl.pallas_call(
        body,
        out_shape=outs,
        in_specs=ins,
        out_specs=[whole() for _ in outs],
        scratch_shapes=list(scratch),
        cost_estimate=pl.CostEstimate(flops=flops, bytes_accessed=moved, transcendentals=0),
        compiler_params=pltpu.CompilerParams(vmem_limit_bytes=limit * MIB),
    )


def to_all(array_in, axes, count):
    copies = jnp.broadcast_to(array_in[None], (count,) + array_in.shape)
    return lax.all_to_all(copies, axes, 0, 0, tiled=True)


def swap(array_in, axis):
    return lax.ppermute(array_in, axis, [(0, 1), (1, 0)])


def in_order(first, mine, other):
    return jnp.where(first, jnp.stack([mine, other]), jnp.stack([other, mine]))


def turn(tile, cosine, sine_low, sine_high):
    return (
        tile * cosine
        + pltpu.roll(tile, 120, 1) * sine_low
        + pltpu.roll(tile, 8, 1) * sine_high
    )


def sine_parts(sine, sign):
    spot = lax.broadcasted_iota(jnp.int32, sine.shape, 1) % 64
    low = jnp.where(spot < 8, -sign * sine, 0.0)
    high = jnp.where((spot >= 8) & (spot < 16), sign * sine, 0.0)
    return low, high


def project_kernel(hidden, gain, shift, weight, bias, cosine, sine, send, normed):
    for block in range(4):
        stream, half_x = block // 2, block % 2
        rows = pl.ds(block * 128, 128)
        moved = hidden[rows, :].astype(F32)
        moved = moved - jnp.mean(moved, axis=1, keepdims=True)
        spread = jnp.mean(moved * moved, axis=1, keepdims=True)
        norm = (moved * lax.rsqrt(spread + EPS) * gain[...] + shift[...]).astype(BF)
        normed[rows, :] = norm
        project = mm(norm, weight[...]) + bias[...]
        cos = cosine[rows, :]
        low, high = sine_parts(sine[rows, :], 1.0)
        left = lax.broadcasted_iota(jnp.int32, (64, 128), 1) < 64
        left_all = lax.broadcasted_iota(jnp.int32, (128, 128), 1) < 64
        for pair in range(2):
            at = pair * 128
            query = turn(project[:, at : at + 128], cos, low, high) * 0.125
            key = turn(project[:, 256 + at : 384 + at], cos, low, high)
            value = project[:, 512 + at : 640 + at]
            q_low, q_high = query[:64], query[64:]
            packed = (
                jnp.where(left, q_low, pltpu.roll(q_high, 64, 1)).astype(BF),
                jnp.where(left, pltpu.roll(q_low, 64, 1), q_high).astype(BF),
            )
            key_value = (
                jnp.where(left_all, key, pltpu.roll(value, 64, 1)).astype(BF),
                jnp.where(left_all, pltpu.roll(key, 64, 1), value).astype(BF),
            )
            for member in range(2):
                head = pair * 2 + member
                for half in range(2):
                    target = stream * 8 + head * 2 + half
                    send[target, pl.ds(half_x * 128, 128), :] = key_value[member]
                    for core in range(2):
                        quarter = half * 2 + core
                        send[target, pl.ds(256 + core * 32 + half_x * 16, 16), :] = packed[member][
                            quarter * 16 : quarter * 16 + 16
                        ]


def mixed_grad_kernel(upstream, weight, send):
    left = lax.broadcasted_iota(jnp.int32, (64, 128), 1) < 64
    for block in range(4):
        stream, half_x = block // 2, block % 2
        grads = mm(upstream[pl.ds(block * 128, 128), :], weight[...], NT)
        for pair in range(2):
            tile = grads[:, pair * 128 : pair * 128 + 128]
            low, high = tile[:64], tile[64:]
            packed = (
                jnp.where(left, low, pltpu.roll(high, 64, 1)).astype(BF),
                jnp.where(left, pltpu.roll(low, 64, 1), high).astype(BF),
            )
            for member in range(2):
                for half in range(2):
                    target = stream * 8 + (pair * 2 + member) * 2 + half
                    for core in range(2):
                        quarter = half * 2 + core
                        send[target, pl.ds(core * 32 + half_x * 16, 16), :] = packed[member][
                            quarter * 16 : quarter * 16 + 16
                        ]


KEY_TILE = 512


def attend_kernel(
    place, block_map, own, other, grad_own, grad_other, out_own, out_other,
    kv, kv_turned, q_grad, scores, chances, key_sums, rows_out,
):
    core, quarter, second, third = place[0], place[1], place[2], place[3]
    left16 = lax.broadcasted_iota(jnp.int32, (16, 128), 1) < 64
    left = lax.broadcasted_iota(jnp.int32, (128, 128), 1) < 64

    def fill(source, grad_source, from_core):
        @pl.loop(0, 32)
        def _(i):
            group, half_x = i // 2, i % 2
            block = block_map[i * 2 + from_core]
            mirror = 127 - block
            kv[pl.ds(mult(block * 64, 64), 64), :] = source[group, pl.ds(mult(half_x * 128, 64), 64), :]
            kv[pl.ds(mult(mirror * 64, 64), 64), :] = source[
                group, pl.ds(mult(half_x * 128 + 64, 64), 64), :
            ]
            spot = core * 32 + half_x * 16
            query = source[group, pl.ds(mult(256 + spot, 16), 16), :].astype(F32)
            grad = grad_source[group, pl.ds(mult(spot, 16), 16), :].astype(F32)
            q_grad[pl.ds(mult(block * 16, 16), 16), :] = jnp.where(
                left16, query, pltpu.roll(grad, 64, 1)
            ).astype(BF)
            q_grad[pl.ds(mult(mirror * 16, 16), 16), :] = jnp.where(
                left16, pltpu.roll(query, 64, 1), grad
            ).astype(BF)

    fill(own, grad_own, core)
    fill(other, grad_other, 1 - core)

    @pl.loop(0, 64)
    def _(c):
        cut = pl.ds(mult(c * 128, 128), 128)
        kv_turned[:, cut] = kv[cut, :].astype(F32).T.astype(BF)
        key_sums[:, cut] = jnp.zeros((128, 128), F32)

    row = lax.broadcasted_iota(jnp.int32, (128, 1), 0)
    offset = (row // 16) * 64 + quarter * 16 + row % 16
    spots = lax.broadcasted_iota(jnp.int32, (128, KEY_TILE), 1)

    def start_of(position):
        return jnp.where(position >= third, third, jnp.where(position >= second, second, 0))

    @pl.loop(0, 16)
    def _(step):
        tile = 15 - step
        rows = pl.ds(mult(tile * 128, 128), 128)
        base = tile * KEY_TILE
        both = q_grad[rows, :]
        query, grad = both[:, :64], both[:, 64:]
        position = base + offset
        first = start_of(position)
        low = start_of(base + quarter * 16) // KEY_TILE
        high = (start_of(base + 448 + quarter * 16 + 15) + KEY_TILE - 1) // KEY_TILE
        high = jnp.minimum(jnp.maximum(high, low), tile)

        def cut_of(j):
            return pl.ds(mult(j * KEY_TILE, KEY_TILE), KEY_TILE)

        def fold(top, part):
            for c in range(KEY_TILE // 128):
                top = jnp.maximum(top, part[:, c * 128 : c * 128 + 128])
            return top

        def plain(j, top):
            part = mm(query, kv_turned[0:64, cut_of(j)])
            scores[:, cut_of(j)] = part
            return fold(top, part)

        def masked(j, top):
            part = mm(query, kv_turned[0:64, cut_of(j)])
            key_at = spots + j * KEY_TILE
            part = jnp.where((key_at <= position) & (key_at >= first), part, NEG_FILL)
            scores[:, cut_of(j)] = part
            return fold(top, part)

        top = jnp.full((128, 128), NEG_FILL, F32)
        top = lax.fori_loop(low, high, masked, top)
        top = lax.fori_loop(high, tile, plain, top)
        top = masked(tile, top)
        row_top = jnp.max(top, axis=1, keepdims=True)

        def weigh(j, state):
            total, mixed = state
            part = jnp.exp(scores[:, cut_of(j)] - row_top)
            for c in range(KEY_TILE // 128):
                total = total + part[:, c * 128 : c * 128 + 128]
            rounded = part.astype(BF)
            chances[:, cut_of(j)] = rounded
            return total, mixed + mm(rounded, kv[cut_of(j), :])

        zero = jnp.zeros((128, 128), F32)
        total, mixed = lax.fori_loop(low, tile + 1, weigh, (zero, zero))
        share = 1.0 / jnp.sum(total, axis=1, keepdims=True)
        mixed = mixed * share
        scaled = jnp.where(left, both.astype(F32), both.astype(F32) * share)
        delta = jnp.sum(jnp.where(left, 0.0, scaled * mixed), axis=1, keepdims=True)
        grad_scaled = scaled[:, 64:].astype(BF)
        turned = scaled.T.astype(BF)
        query_turned, grad_turned = turned[:64], turned[64:]

        def back(j, query_sum):
            cut = cut_of(j)
            part = chances[:, cut]
            along = mm(grad_scaled, kv_turned[64:128, cut])
            score_grad = (part.astype(F32) * (along - delta)).astype(BF)
            key_sums[0:64, cut] += mm(query_turned, score_grad)
            key_sums[64:128, cut] += mm(grad_turned, part)
            return query_sum + mm(score_grad, kv[cut, :])

        query_sum = lax.fori_loop(low, tile + 1, back, zero)
        rows_out[rows, :] = jnp.where(left, query_sum * 0.125, mixed).astype(BF)

    @pl.loop(0, 64)
    def _(c):
        cut = pl.ds(mult(c * 128, 128), 128)
        kv[cut, :] = key_sums[:, cut].T.astype(BF)

    def spill(target, to_core):
        @pl.loop(0, 32)
        def _(i):
            group, half_x = i // 2, i % 2
            block = block_map[i * 2 + to_core]
            mirror = 127 - block
            target[group, pl.ds(mult(half_x * 128, 64), 64), :] = kv[pl.ds(mult(block * 64, 64), 64), :]
            target[group, pl.ds(mult(half_x * 128 + 64, 64), 64), :] = kv[
                pl.ds(mult(mirror * 64, 64), 64), :
            ]
            spot = 256 + half_x * 32
            target[group, pl.ds(mult(spot, 16), 16), :] = rows_out[pl.ds(mult(block * 16, 16), 16), :]
            target[group, pl.ds(mult(spot + 16, 16), 16), :] = rows_out[
                pl.ds(mult(mirror * 16, 16), 16), :
            ]

    spill(out_own, core)
    spill(out_other, 1 - core)


def collect_kernel(place, back, cosine, sine, project_grad, mixed_out, heads):
    core = place[0]
    left = lax.broadcasted_iota(jnp.int32, (128, 128), 1) < 64
    for block in range(4):
        stream, half_x = block // 2, block % 2
        rows = pl.ds(block * 128, 128)
        cos = cosine[rows, :]
        low, high = sine_parts(sine[rows, :], -1.0)
        for pair in range(2):
            pieces = []
            for member in range(2):
                base = stream * 8 + (pair * 2 + member) * 2
                cut = pl.ds(half_x * 128, 128)
                key_value = back[base, cut, :].astype(F32) + back[base + 1, cut, :].astype(F32)
                for upper in range(2):
                    for half in range(2):
                        for of_core in range(2):
                            flipped = of_core ^ core
                            spot = 256 + flipped * 64 + (half_x * 2 + upper) * 16
                            heads[
                                member, pl.ds(upper * 64 + (half * 2 + of_core) * 16, 16), :
                            ] = back[base + half, pl.ds(mult(spot, 16), 16), :]
                pieces.append((heads[member].astype(F32), key_value))
            (row0, kv0), (row1, kv1) = pieces
            at = pair * 128
            query = jnp.where(left, row0, pltpu.roll(row1, 64, 1))
            key = jnp.where(left, kv0, pltpu.roll(kv1, 64, 1))
            value = jnp.where(left, pltpu.roll(kv0, 64, 1), kv1)
            mixed = jnp.where(left, pltpu.roll(row0, 64, 1), row1)
            project_grad[rows, at : at + 128] = turn(query, cos, low, high).astype(BF)
            project_grad[rows, 256 + at : 384 + at] = turn(key, cos, low, high).astype(BF)
            project_grad[rows, 512 + at : 640 + at] = value.astype(BF)
            mixed_out[rows, at : at + 128] = mixed.astype(BF)


def feed_weights_kernel(place, normed, inner_grad, active, upstream, out_own, out_other):
    for flip, target in ((0, out_own), (1, out_other)):
        core = place[0] ^ flip
        for part in range(2):
            rows = normed[:, pl.ds(mult(part * 512 + core * 256, 256), 256)]
            for quad in range(4):
                grads = mm(rows, inner_grad[:, quad * 256 : quad * 256 + 256], TN).astype(BF)
                for n in range(2):
                    slot = part * 8 + quad * 2 + n
                    target[:, slot * 16 : slot * 16 + 16, :] = grads[:, n * 128 : n * 128 + 128].reshape(
                        16, 16, 128
                    )
        rows = active[:, pl.ds(mult(core * 512, 512), 512)]
        for quad in range(4):
            grads = mm(rows, upstream[:, quad * 256 : quad * 256 + 256], TN).astype(BF)
            for n in range(2):
                at = 256 + (quad * 2 + n) * 32
                target[:, at : at + 32, :] = grads[:, n * 128 : n * 128 + 128].reshape(16, 32, 128)


def attend_weights_kernel(place, normed, project_grad, mixed, upstream, out_own, out_other):
    for flip, target in ((0, out_own), (1, out_other)):
        core = place[0] ^ flip
        for part in range(2):
            rows = normed[:, pl.ds(mult(part * 512 + core * 256, 256), 256)]
            for block in range(3):
                grads = mm(rows, project_grad[:, block * 256 : block * 256 + 256], TN).astype(BF)
                for n in range(2):
                    slot = part * 6 + block * 2 + n
                    target[:, slot * 16 : slot * 16 + 16, :] = grads[:, n * 128 : n * 128 + 128].reshape(
                        16, 16, 128
                    )
        for block in range(2):
            columns = upstream[:, pl.ds(mult(core * 512 + block * 256, 256), 256)]
            grads = mm(mixed[...], columns, TN).astype(BF)
            for n in range(2):
                at = 192 + (block * 2 + n) * 16
                target[:, at : at + 16, :] = grads[:, n * 128 : n * 128 + 128].reshape(16, 16, 128)


def spread_kernel(place, mine, other, out, *, columns):
    here = pl.program_id(0) == 0

    def put(source):
        for at, chip, slot, count in columns:
            out[:, at : at + 128] = source[0, chip, slot : slot + count, :].astype(F32)

    @pl.when(here)
    def _():
        put(mine)

    @pl.when(jnp.logical_not(here))
    def _():
        put(other)


def spread(place, mine, other, rows, width, columns):
    shape = (1,) + mine.shape[1:]
    return pl.pallas_call(
        functools.partial(spread_kernel, columns=columns),
        out_shape=jax.ShapeDtypeStruct((32 * rows, width), F32),
        grid_spec=pltpu.PrefetchScalarGridSpec(
            num_scalar_prefetch=1,
            grid=(2, 16),
            in_specs=[
                pl.BlockSpec(shape, lambda a, g, place: (jnp.where(a == 0, g, 15), 0, 0, 0)),
                pl.BlockSpec(shape, lambda a, g, place: (jnp.where(a == 0, 0, g), 0, 0, 0)),
            ],
            out_specs=pl.BlockSpec(
                (rows, width), lambda a, g, place: ((place[0] ^ a) * 16 + g, 0)
            ),
        ),
        cost_estimate=pl.CostEstimate(
            flops=0, bytes_accessed=32 * rows * width * 6, transcendentals=0
        ),
        compiler_params=pltpu.CompilerParams(vmem_limit_bytes=32 * MIB),
    )(place, mine, other)


def shape(*sizes, dtype=BF):
    return jax.ShapeDtypeStruct(sizes, dtype)


def normalized(hidden):
    moved = hidden - jnp.mean(hidden, axis=-1, keepdims=True)
    spread_out = jnp.mean(moved * moved, axis=-1, keepdims=True)
    scale = lax.rsqrt(spread_out + EPS)
    return moved * scale, scale


def per_device(
    hidden_in, doc_ids, block_map, attn_gain, attn_shift, mlp_gain, mlp_shift, qkv_weight, qkv_bias,
    out_weight, out_bias, in_weight, in_bias, proj_weight, proj_bias, cotangent,
):
    y, z = lax.axis_index("y"), lax.axis_index("z")
    xh, xl = lax.axis_index("xh"), lax.axis_index("xl")
    core = lax.axis_index("core")
    group = y * 4 + z
    chip = xh * 2 + xl
    low_half = xh == 0
    smem = whole(pltpu.SMEM)

    hidden = to_all(hidden_in[0], RING, 4).reshape(512, 1024)

    segment = doc_ids[0]
    bounds = jnp.stack([jnp.sum((segment < label).astype(jnp.int32)) for label in (1, 2)])
    bound_parts = jnp.stack([bounds // 128, bounds % 128]).reshape(4).astype(BF)
    vectors = jnp.concatenate(
        [attn_gain, attn_shift, mlp_gain, mlp_shift, qkv_bias, in_bias, out_bias, proj_bias,
         bound_parts, jnp.zeros((508,), BF)]
    ).reshape(56, 128)
    vectors_other = swap(vectors, "xh")

    chunk = (core * 16 + group) * 16
    partner = (1 - xh) * 2 + xl

    def weight_columns(which, first_row, rows):
        return jnp.concatenate(
            [lax.dynamic_slice(qkv_weight, (first_row, k * 1024 + which * 256), (rows, 256)) for k in range(3)]
            + [lax.dynamic_slice(in_weight, (first_row, which * 1024), (rows, 1024))],
            axis=1,
        )

    piece = swap(weight_columns(partner, chunk, 16), "xh")
    piece = to_all(piece, PLANE, 16).reshape(256, 1792)
    others = in_order(core == 0, piece, swap(piece, "core")).reshape(512, 1792)
    weights = in_order(low_half, weight_columns(chip, 0, 512), others).reshape(1024, 1792)
    qkv_here, in_here = weights[:, :768], weights[:, 768:]

    pairs = in_order(low_half, vectors.reshape(-1), vectors_other.reshape(-1))
    a_gain = pairs[:, 0:512].reshape(1, 1024).astype(F32)
    a_shift = pairs[:, 512:1024].reshape(1, 1024).astype(F32)
    m_gain = pairs[:, 1024:1536].reshape(1, 1024).astype(F32)
    m_shift = pairs[:, 1536:2048].reshape(1, 1024).astype(F32)
    qkv_bias_all = pairs[:, 2048:3584].reshape(3, 1024).astype(F32)
    qkv_bias_here = lax.dynamic_slice(qkv_bias_all, (0, chip * 256), (3, 256)).reshape(1, 768)
    in_bias_here = lax.dynamic_slice(
        pairs[:, 3584:5632].reshape(1, 4096), (0, chip * 1024), (1, 1024)
    ).astype(F32)
    branch_bias = (
        pairs[:, 5632:6144].reshape(1, 1024).astype(F32) + pairs[:, 6144:6656].reshape(1, 1024).astype(F32)
    )
    bound_pairs = pairs[:, 6656:6660].astype(F32).astype(jnp.int32)
    doc_bounds = bound_pairs[:, 0:2] * 128 + bound_pairs[:, 2:4]

    places = (group * 2 + jnp.arange(2, dtype=jnp.int32)) * 2 + core
    blocks = jnp.take(block_map, places)
    steps = jnp.arange(64, dtype=jnp.int32)
    position = jnp.stack(
        [blocks[:, None] * 64 + steps[None], (127 - blocks)[:, None] * 64 + steps[None]], axis=1
    ).reshape(1, 256)
    second, third = doc_bounds[:, 0:1], doc_bounds[:, 1:2]
    first = jnp.where(position >= third, third, jnp.where(position >= second, second, 0))
    relative = (position - first).astype(F32).reshape(512, 1)
    frequency = 10000.0 ** (-(jnp.arange(0, ROT, 2).astype(F32) / ROT))
    lanes = jnp.concatenate([frequency, frequency, jnp.zeros((48,), F32)])
    angles = relative * jnp.concatenate([lanes, lanes])[None]
    cosine, sine = jnp.cos(angles), jnp.sin(angles)

    cotangent, hidden = lax.optimization_barrier((cotangent, hidden))
    upstream = to_all(cotangent[0], RING, 4).reshape(512, 1024)

    send, normed = call(
        project_kernel,
        [shape(16, 320, 128), shape(512, 1024)],
        [whole()] * 7,
        flops=2 * 512 * 1024 * 768,
        moved=6 * MIB,
    )(hidden, a_gain, a_shift, qkv_here, qkv_bias_here, cosine, sine)
    heads_own = lax.all_to_all(send, PLANE, 0, 0, tiled=True)
    heads_other = swap(heads_own, "core")

    out_here = lax.dynamic_slice(out_weight, (xl * 256, 0), (256, 1024))
    (grad_send,) = call(
        mixed_grad_kernel, [shape(16, 64, 128)], [whole()] * 2, flops=2 * 512 * 1024 * 256, moved=2 * MIB
    )(upstream, out_here)
    grads_own = lax.all_to_all(grad_send, PLANE, 0, 0, tiled=True)
    grads_other = swap(grads_own, "core")

    hidden_full = hidden.astype(F32)
    xhat, _ = normalized(hidden_full)
    normed_mlp = (xhat * m_gain + m_shift).astype(BF)
    inner = mm(normed_mlp, in_here) + in_bias_here
    bell = 0.5 * (1.0 + lax.erf(inner * (2.0**-0.5)))
    active = (inner * bell).astype(BF)
    proj_here = lax.dynamic_slice(proj_weight, (xl * 1024, 0), (1024, 1024))
    branch_mlp = mm(active, proj_here)
    active_grad = mm(upstream, proj_here, NT)
    slope = bell + inner * jnp.exp(-0.5 * inner * inner) * (1.0 / math.sqrt(2.0 * math.pi))
    inner_grad = (active_grad * slope).astype(BF)
    normed_mlp_grad = mm(inner_grad, in_here, NT)

    core_at = core.astype(jnp.int32).reshape(1)
    feed_own, feed_other = call(
        feed_weights_kernel,
        [shape(16, 512, 128)] * 2,
        [smem] + [whole()] * 4,
        flops=4 * 512 * 1024 * 1024,
        moved=8 * MIB,
    )(core_at, normed_mlp, inner_grad, active, upstream)

    def reduce_plane(own, other):
        both = own + swap(other, "core")
        parts = lax.all_to_all(both, PLANE, 0, 0, tiled=True)
        return jnp.sum(parts.astype(F32), axis=0).astype(BF)

    feed = reduce_plane(feed_own, feed_other)
    in_part = lax.all_to_all(
        jnp.broadcast_to(feed[:256].reshape(2, 1, 128, 128), (2, 2, 128, 128)).reshape(4, 128, 128),
        RING, 0, 0, tiled=True,
    )
    proj_part = in_order(xl == 0, feed[256:], swap(feed[256:], "xl"))
    feed_all = to_all(
        jnp.concatenate([in_part.reshape(512, 128), proj_part.reshape(512, 128)]), PLANE, 16
    )
    feed_core = swap(feed_all, "core")

    quarter = (group % 2) * 2 + core
    here = lax.dynamic_index_in_dim(doc_bounds, group // 8, 0, keepdims=False)
    place = jnp.concatenate([core_at, quarter.astype(jnp.int32).reshape(1), here])
    back_own, back_other = call(
        attend_kernel,
        [shape(16, 320, 128)] * 2,
        [smem, smem] + [whole()] * 4,
        scratch=[
            pltpu.VMEM((8192, 128), BF),
            pltpu.VMEM((128, 8192), BF),
            pltpu.VMEM((2048, 128), BF),
            pltpu.VMEM((128, 8192), F32),
            pltpu.VMEM((128, 8192), BF),
            pltpu.VMEM((128, 8192), F32),
            pltpu.VMEM((2048, 128), BF),
        ],
        flops=2 * 4 * 6 * 64 * 4 * MIB,
        moved=6 * MIB,
    )(place, block_map, heads_own, heads_other, grads_own, grads_other)

    arrived = swap(back_other, "core")
    returned = lax.all_to_all(
        jnp.concatenate(
            [back_own[:, :256] + arrived[:, :256], back_own[:, 256:], arrived[:, 256:]], axis=1
        ),
        PLANE, 0, 0, tiled=True,
    )
    project_grad, mixed = call(
        collect_kernel,
        [shape(512, 768), shape(512, 256)],
        [smem] + [whole()] * 3,
        scratch=[pltpu.VMEM((2, 128, 128), BF)],
        moved=3 * MIB,
    )(core_at, returned, cosine, sine)

    heads_grad_own, heads_grad_other = call(
        attend_weights_kernel,
        [shape(16, 256, 128)] * 2,
        [smem] + [whole()] * 4,
        flops=2 * 512 * 1024 * 1024,
        moved=6 * MIB,
    )(core_at, normed, project_grad, mixed, upstream)
    heads_sum = reduce_plane(heads_grad_own, heads_grad_other)
    qkv_part = lax.all_to_all(
        jnp.broadcast_to(heads_sum[:192].reshape(2, 1, 96, 128), (2, 2, 96, 128)).reshape(4, 96, 128),
        RING, 0, 0, tiled=True,
    )
    out_part = in_order(xl == 0, heads_sum[192:], swap(heads_sum[192:], "xl"))
    heads_all = to_all(
        jnp.concatenate([qkv_part.reshape(384, 128), out_part.reshape(128, 128)]), PLANE, 16
    )
    heads_core = swap(heads_all, "core")

    branch = branch_mlp + mm(mixed, out_here)
    normed_grad = mm(project_grad, qkv_here, NT)
    entry = normed_grad * a_gain + normed_mlp_grad * m_gain
    ring_rows = lax.all_to_all(
        jnp.concatenate([branch.reshape(4, 128, 1024), entry.reshape(4, 128, 1024)], axis=1).astype(BF),
        RING, 0, 0, tiled=True,
    )
    ring_rows = jnp.sum(ring_rows.astype(F32), axis=0)
    own_hidden = hidden_in[0].astype(F32)
    own_upstream = cotangent[0].astype(F32)
    hidden_out = (own_hidden + ring_rows[:128] + branch_bias).astype(BF)[None]
    own_xhat, own_scale = normalized(own_hidden)
    own_entry = ring_rows[128:]
    hidden_grad = (
        own_upstream
        + own_scale
        * (
            own_entry
            - jnp.mean(own_entry, axis=1, keepdims=True)
            - own_xhat * jnp.mean(own_entry * own_xhat, axis=1, keepdims=True)
        )
    )[None]

    def column_sum(array_in):
        return jnp.sum(array_in.astype(F32), axis=0)

    small = jnp.concatenate(
        [
            column_sum(normed_grad * xhat),
            column_sum(normed_grad),
            column_sum(normed_mlp_grad * xhat),
            column_sum(normed_mlp_grad),
            column_sum(own_upstream),
            column_sum(project_grad),
            column_sum(inner_grad),
            jnp.zeros((256,), F32),
        ]
    ).reshape(56, 128)
    small = small + swap(small, "core")
    small = jnp.sum(to_all(small, PLANE, 16), axis=0)
    small = to_all(small, RING, 4)
    common = jnp.sum(small[:, :40], axis=0).reshape(5, 1024)
    common = lax.dynamic_slice(common, (0, xh * 512), (5, 512))
    qkv_bias_grad = small[:, 40:46].reshape(4, 3, 256).transpose(1, 0, 2).reshape(3072)
    qkv_bias_grad = lax.dynamic_slice(qkv_bias_grad, (xh * 1536,), (1536,))
    in_bias_grad = lax.dynamic_slice(small[:, 46:54].reshape(4096), (xh * 2048,), (2048,))

    qkv_columns = [
        ((n // 2) * 1024 + c * 256 + (n % 2) * 128, c, n * 16, 16) for c in range(4) for n in range(6)
    ]
    in_columns = [(c * 1024 + n * 128, c, n * 16, 16) for c in range(4) for n in range(8)]

    def pieces(gathered, first_row, rows, chips):
        return gathered[:, first_row : first_row + rows].reshape(16, chips, rows // chips, 128)

    qkv_weight_grad = spread(
        core_at, pieces(heads_all, 0, 384, 4), pieces(heads_core, 0, 384, 4), 16, 3072, qkv_columns
    )
    in_weight_grad = spread(
        core_at, pieces(feed_all, 0, 512, 4), pieces(feed_core, 0, 512, 4), 16, 4096, in_columns
    )
    proj_own = pieces(feed_all, 512, 512, 2)
    proj_core = pieces(feed_core, 512, 512, 2)
    proj_both = in_order(core == 0, proj_own, proj_core).reshape(2, 16, 2, 8, 32, 128)
    proj_weight_grad = proj_both.transpose(2, 0, 1, 4, 3, 5).reshape(2048, 1024).astype(F32)
    out_own = pieces(heads_all, 384, 128, 2)
    out_core = pieces(heads_core, 384, 128, 2)
    out_both = in_order(core == 0, out_own, out_core).reshape(2, 16, 2, 4, 16, 128)
    out_weight_grad = out_both.transpose(2, 1, 4, 0, 3, 5).reshape(512, 1024).astype(F32)

    return (
        hidden_out, hidden_grad, common[0], common[1], common[2], common[3], qkv_weight_grad,
        qkv_bias_grad, out_weight_grad, common[4], in_weight_grad, in_bias_grad, proj_weight_grad,
        common[4],
    )


def solution(mesh):
    fine = Mesh(mesh.devices.reshape(4, 4, 2, 2, 2), ("y", "z", "xl", "core", "xh"))
    ctx = ("y", "z", "xl", "core")
    rows = P("xh", ctx, None)
    half = P("xh")
    wide = P("xh", None)
    in_specs = (
        rows, wide, P(), half, half, half, half, wide, half, wide, half, wide, half, wide, half, rows,
    )
    out_specs = (
        rows, rows, half, half, half, half, wide, half, wide, half, wide, half, wide, half,
    )
    return jax.shard_map(
        per_device, mesh=fine, in_specs=in_specs, out_specs=out_specs, check_vma=False
    )
```

time: 2630 us -> 543 us (0.21)
  waiting for transfers between devices: 1280 us -> 215 us
  blocking collectives: 616 us -> 14.7 us
  matrix products: 342 us -> 18.8 us
  local copies, waits for them, and re-layouts: 268 us -> 56.2 us
  Pallas kernels: 0 us -> 118 us
  starting transfers between devices: 0.83 us -> 77.1 us
  other arithmetic: 93.4 us -> 30.2 us
    reduce_scatter x5 -> x0, waiting for transfers between devices: 939 us -> none  [the longest x1 670 us: per_device(): lax.psum_scatter(grad_terms, 'ctx', scatter_dimension=0, tiled=True)]
    psum x1 -> x0, blocking collectives: 557 us -> none  [per_device(): lax.psum((summed[0], summed[1], summed[2], summed[3], summed[4], summed[5...]
    all_gather x6 -> x0, waiting for transfers between devices: 340 us -> none  [the longest x1 142 us: per_device(): lax.all_gather(values_here.reshape(row_count, width_all), 'ctx', axis=0,...]
    dot_general x68 -> x6, matrix products: 342 us -> 18.8 us  [mm(): return lax.dot_general(left, right, dims, preferred_element_type=F32)]
    all_to_all x0 -> x14, waiting for transfers between devices: none -> 190 us  [the longest x6 113 us: to_all(): return lax.all_to_all(copies, axes, 0, 0, tiled=True)]
    dynamic_update_slice x16 -> x0, local copies, waits for them, and re-layouts: 135 us -> none  [attend_back(): lax.scan(scan_back, jnp.zeros(queries.shape, jnp.float32), stacked)]
    pallas_call x0 -> x8, Pallas kernels: none -> 118 us  [the longest x1 83.2 us: per_device(): call(attend_kernel, [shape(16, 320, 128)] * 2, [smem, smem] + [whole()] *...]
    all_to_all x0 -> x14, starting transfers between devices: none -> 69 us  [the longest x6 33.4 us: to_all(): return lax.all_to_all(copies, axes, 0, 0, tiled=True)]
  transfers between devices with their start and end apart: 11 -> 27, of which waited for: 8 -> 16; matrix products, arithmetic and copies ran while one was open for 27% -> 13% of each run, Pallas kernels for 0% -> 4%
where the time goes in v1:
time: 543 us; the launch traced here: 533 us
  waiting for transfers between devices  215 us (40%)
  Pallas kernels  118 us (22%)
  starting transfers between devices  77.1 us (14%)
  local copies, waits for them, and re-layouts  56.2 us (10%)
  other arithmetic  30.2 us (6%)
  matrix products  18.8 us (3%)
  blocking collectives  14.7 us (3%)
    all_to_all x6, waiting for transfers between devices, to_all(): return lax.all_to_all(copies, axes, 0, 0, tiled=True)  113 us
    pallas_call x1, Pallas kernels, per_device(): call(attend_kernel, [shape(16, 320, 128)] * 2, [smem, smem] + [whole()] *...  83.2 us
    all_to_all x6, starting transfers between devices, to_all(): return lax.all_to_all(copies, axes, 0, 0, tiled=True)  33.4 us
    all_to_all x2, waiting for transfers between devices, reduce_plane(): parts = lax.all_to_all(both, PLANE, 0, 0, tiled=True)  25 us
    ppermute x13, waiting for transfers between devices, swap(): return lax.ppermute(array_in, axis, [(0, 1), (1, 0)])  24.9 us
    pallas_call x2, Pallas kernels, spread(): pl.pallas_call(functools.partial(spread_kernel, columns=columns), out_sha...  22.8 us
    all_to_all x1, waiting for transfers between devices, per_device(): lax.all_to_all(jnp.concatenate([back_own[:, :256] + arrived[:, :256], bac...  20.8 us
    dot_general x6, matrix products, mm(): return lax.dot_general(left, right, dims, preferred_element_type=F32)  18.8 us
  transfers between devices with their start and end apart: 27, of which 16 were waited for; matrix products, arithmetic and copies ran while one was open for 13% of the time, Pallas kernels for 4%

profile of v1, /device:TPU:0, one launch (start us, length us, event | category | flops | bytes accessed | tf_op | source)
XLA Modules:
  0.0 532.6 jit_solution(4848511475686982940)
XLA Ops:
  3.7 5.6 %concatenate.75 = bf16[7168]{0:T(1024)(128)(2,1)S(1)} concatenate(bf16[512]{0:T(512)(128)(2,1)} %param.19, bf16[512]{0:T(512)(128)(2,1)} %param.20, bf16[512]{0:T(512)(128)(2,1)} %param.21, bf16[512]{0:T(512)(128)(2,1)} %param.22, bf16[1536]{0:T(1024)(128)(2,1)} %param.24, bf16[2048]{0:T(1024)(128)(2,1)} %param.28, bf16[512]{0:T(512)(128)(2,1)} %param.26, bf16[512]{0:T(512)(128)(2,1)} %param.30, ...), dimensions={0} | concatenate | bytes 28672 | tf_op jit(solution)/shard_map/concatenate | solution.py:424
  9.3 3.1 collective-permute-start
  21.0 8.1 %all-to-all-start.1 = ((bf16[16,16,1792]{2,1,0:T(8,128)(2,1)}), bf16[16,16,1792]{2,1,0:T(8,128)(2,1)S(1)}, u32[]{:S(2)}, u32[]{:S(2)}) async-start(bf16[16,16,1792]{2,1,0:T(8,128)(2,1)} %broadcast_in_dim.54), calls=%async_computation.1 | async-start | bytes 1835008 | tf_op jit(solution)/shard_map/all_to_all | solution.py:52
  29.8 14.4 %all-to-all-done.1 = bf16[16,16,1792]{2,1,0:T(8,128)(2,1)S(1)} async-done(((bf16[16,16,1792]{2,1,0:T(8,128)(2,1)}), bf16[16,16,1792]{2,1,0:T(8,128)(2,1)S(1)}, u32[]{:S(2)}, u32[]{:S(2)}) %all-to-all-start.1) | async-done | bytes 917536 | tf_op jit(solution)/shard_map/all_to_all | solution.py:52
  45.3 4.3 all-to-all-start
  51.9 10.7 %all-to-all-done = bf16[4,128,1024]{2,1,0:T(8,128)(2,1)S(1)} async-done(((bf16[4,128,1024]{2,1,0:T(8,128)(2,1)}), bf16[4,128,1024]{2,1,0:T(8,128)(2,1)S(1)}, u32[]{:S(2)}, u32[]{:S(2)}) %all-to-all-start) | async-done | bytes 1048608 | tf_op jit(solution)/shard_map/all_to_all | solution.py:52
  71.2 4.5 all-to-all-start.2
  75.8 17.7 %all-to-all-done.2.own = bf16[16,320,128]{2,1,0:T(8,128)(2,1)} async-done(((bf16[16,320,128]{2,1,0:T(8,128)(2,1)}), bf16[16,320,128]{2,1,0:T(8,128)(2,1)}, u32[]{:S(2)}, u32[]{:S(2)}) %all-to-all-start.2) | async-done | bytes 1310752 | tf_op jit(solution)/shard_map/all_to_all | solution.py:486
  94.6 3.5 all-to-all-start.3
  99.1 10.8 %all-to-all-done.3 = bf16[4,128,1024]{2,1,0:T(8,128)(2,1)S(1)} async-done(((bf16[4,128,1024]{2,1,0:T(8,128)(2,1)}), bf16[4,128,1024]{2,1,0:T(8,128)(2,1)S(1)}, u32[]{:S(2)}, u32[]{:S(2)}) %all-to-all-start.3) | async-done | bytes 1048608 | tf_op jit(solution)/shard_map/all_to_all | solution.py:52
  111.5 6.0 %all-to-all-start.4 = ((bf16[16,64,128]{2,1,0:T(8,128)(2,1)}), bf16[16,64,128]{2,1,0:T(8,128)(2,1)S(1)}, u32[]{:S(2)}, u32[]{:S(2)}) async-start(bf16[16,64,128]{2,1,0:T(8,128)(2,1)} %shard_map.264), calls=%async_computation.4 | async-start | bytes 524288 | tf_op jit(solution)/shard_map/all_to_all | solution.py:493
  117.8 8.3 %all-to-all-done.4.grad_own = bf16[16,64,128]{2,1,0:T(8,128)(2,1)S(1)} async-done(((bf16[16,64,128]{2,1,0:T(8,128)(2,1)}), bf16[16,64,128]{2,1,0:T(8,128)(2,1)S(1)}, u32[]{:S(2)}, u32[]{:S(2)}) %all-to-all-start.4) | async-done | bytes 262176 | tf_op jit(solution)/shard_map/all_to_all | solution.py:493
  127.6 83.2 %shard_map.265 = (bf16[16,320,128]{2,1,0:T(8,128)(2,1)S(1)}, bf16[16,320,128]{2,1,0:T(8,128)(2,1)S(1)}) custom-call(s32[4]{0:T(128)S(1)} %pad_add_fusion.2.place, s32[64]{0:T(128)S(1)} %copy-done.2, bf16[16,320,128]{2,1,0:T(8,128)(2,1)} %all-to-all-done.2.own, bf16[16,320,128]{2,1,0:T(8,128)(2,1)} %collective-permute-done.3.other, ...), custom_call_target="tpu_custom_call" | custom-call | flops 12884901888 | bytes 6291456 | tf_op jit(solution)/shard_map/pallas_call | solution.py:537
  214.1 2.7 convert_reduce_fusion.2
  216.8 4.1 shard_map.269
  222.7 4.4 all-to-all-start.5
  227.1 4.1 add.387
  231.2 20.8 %all-to-all-done.5.back = bf16[16,384,128]{2,1,0:T(8,128)(2,1)} async-done(((bf16[16,384,128]{2,1,0:T(8,128)(2,1)}), bf16[16,384,128]{2,1,0:T(8,128)(2,1)}, u32[]{:S(2)}, u32[]{:S(2)}) %all-to-all-start.5) | async-done | bytes 1572896 | tf_op jit(solution)/shard_map/all_to_all | solution.py:555
  252.0 4.4 all-to-all-start.12
  256.4 2.6 shard_map.266
  262.3 4.2 fusion.23
  266.5 18.9 %all-to-all-done.12 = bf16[16,512,128]{2,1,0:T(8,128)(2,1)} async-done(((bf16[16,512,128]{2,1,0:T(8,128)(2,1)}), bf16[16,512,128]{2,1,0:T(8,128)(2,1)}, u32[]{:S(2)}, u32[]{:S(2)}) %all-to-all-start.12) | async-done | bytes 2097184 | tf_op jit(solution)/shard_map/all_to_all | solution.py:520
  288.7 3.3 all-to-all-start.13
  292.0 4.1 fusion.49
  296.1 2.5 add.385
  298.6 4.5 all-to-all-start.9
  305.7 4.0 fusion.51
  311.2 6.1 %all-to-all-done.9 = bf16[16,256,128]{2,1,0:T(8,128)(2,1)} async-done(((bf16[16,256,128]{2,1,0:T(8,128)(2,1)}), bf16[16,256,128]{2,1,0:T(8,128)(2,1)}, u32[]{:S(2)}, u32[]{:S(2)}) %all-to-all-start.9) | async-done | bytes 1048608 | tf_op jit(solution)/shard_map/all_to_all | solution.py:520
  317.3 4.5 all-to-all-start.6
  323.8 19.1 %collective-permute-done.11 = bf16[256,128]{1,0:T(8,128)(2,1)S(1)} collective-permute-done((bf16[256,128]{1,0:T(8,128)(2,1)S(1)}, bf16[256,128]{1,0:T(8,128)(2,1)S(1)}, u32[]{:S(2)}, u32[]{:S(2)}) %collective-permute-start.11) | collective-permute-done | bytes 65568 | tf_op jit(solution)/shard_map/ppermute | solution.py:56
  344.9 3.9 all-to-all-start.10
  348.9 5.8 %all-to-all-done.10 = bf16[4,96,128]{2,1,0:T(8,128)(2,1)S(1)} async-done(((bf16[4,96,128]{2,1,0:T(8,128)(2,1)}), bf16[4,96,128]{2,1,0:T(8,128)(2,1)S(1)}, u32[]{:S(2)}, u32[]{:S(2)}) %all-to-all-start.10) | async-done | bytes 98336 | tf_op jit(solution)/shard_map/all_to_all | solution.py:577
  354.6 2.8 broadcast_in_dim.117
  357.5 6.5 %all-to-all-start.14 = ((bf16[16,1024,128]{2,1,0:T(8,128)(2,1)}), bf16[16,1024,128]{2,1,0:T(8,128)(2,1)}, u32[]{:S(2)}, u32[]{:S(2)}) async-start(bf16[16,1024,128]{2,1,0:T(8,128)(2,1)} %broadcast_in_dim.117), calls=%async_computation.14 | async-start | bytes 8388608 | tf_op jit(solution)/shard_map/all_to_all | solution.py:52
  364.8 3.2 collective-permute-done.8
  368.0 44.5 %all-to-all-done.14 = bf16[16,1024,128]{2,1,0:T(8,128)(2,1)} async-done(((bf16[16,1024,128]{2,1,0:T(8,128)(2,1)}), bf16[16,1024,128]{2,1,0:T(8,128)(2,1)}, u32[]{:S(2)}, u32[]{:S(2)}) %all-to-all-start.14) | async-done | bytes 4194336 | tf_op jit(solution)/shard_map/all_to_all | solution.py:52
  414.2 7.4 %all-to-all-start.11 = ((bf16[16,512,128]{2,1,0:T(8,128)(2,1)}), bf16[16,512,128]{2,1,0:T(8,128)(2,1)}, u32[]{:S(2)}, u32[]{:S(2)}) async-start(bf16[16,512,128]{2,1,0:T(8,128)(2,1)} %broadcast_in_dim.114), calls=%async_computation.11 | async-start | bytes 4194304 | tf_op jit(solution)/shard_map/all_to_all | solution.py:52
  423.5 26.5 %all-to-all-done.11 = bf16[16,512,128]{2,1,0:T(8,128)(2,1)} async-done(((bf16[16,512,128]{2,1,0:T(8,128)(2,1)}), bf16[16,512,128]{2,1,0:T(8,128)(2,1)}, u32[]{:S(2)}, u32[]{:S(2)}) %all-to-all-start.11) | async-done | bytes 2097184 | tf_op jit(solution)/shard_map/all_to_all | solution.py:52
  454.3 14.7 %all_to_all.75 = f32[16,56,128]{2,1,0:T(8,128)S(1)} all-to-all(f32[16,56,128]{2,1,0:T(8,128)S(1)} %broadcast_in_dim.62), channel_id=1, replica_groups=mesh['y'=4,'z'=4,'xl'=2,'core'=2,'xh'=2] {'y','z'}, dimensions={0} | all-to-all | bytes 917504 | tf_op jit(solution)/shard_map/all_to_all | solution.py:52
  469.7 3.5 all-to-all-start.8
  473.2 5.8 %all-to-all-done.8 = f32[4,56,128]{2,1,0:T(8,128)S(1)} async-done(((f32[4,56,128]{2,1,0:T(8,128)}), f32[4,56,128]{2,1,0:T(8,128)S(1)}, u32[]{:S(2)}, u32[]{:S(2)}) %all-to-all-start.8) | async-done | bytes 114720 | tf_op jit(solution)/shard_map/all_to_all | solution.py:52
  481.1 2.6 fusion.53
  487.3 2.7 slice.187
  493.7 3.0 reshape.679
  498.6 11.2 %shard_map.268 = f32[512,3072]{1,0:T(8,128)} custom-call(s32[1]{0:T(128)} %bitcast.12.place, bf16[16,4,96,128]{3,2,1,0:T(8,128)(2,1)S(1)} %bitcast.134, bf16[16,4,96,128]{3,2,1,0:T(8,128)(2,1)S(1)} %bitcast.135), custom_call_target="tpu_custom_call" | custom-call | bytes 9437184 | tf_op jit(solution)/shard_map/pallas_call | solution.py:375
  509.8 2.5 fusion.54
  514.7 5.5 %copy.84 = f32[256,8,8,128]{3,1,2,0:T(8,128)} copy(f32[256,8,8,128]{3,2,1,0:T(8,128)S(1)} %bitcast.143) | data formatting | bytes 16777216
  520.1 11.6 %shard_map.270 = f32[512,4096]{1,0:T(8,128)} custom-call(s32[1]{0:T(128)} %bitcast.12.place, bf16[16,4,128,128]{3,2,1,0:T(8,128)(2,1)S(1)} %bitcast.132, bf16[16,4,128,128]{3,2,1,0:T(8,128)(2,1)S(1)} %bitcast.133), custom_call_target="tpu_custom_call" | custom-call | bytes 12582912 | tf_op jit(solution)/shard_map/pallas_call | solution.py:375
  (230 shorter events, 72.5 us)
Async XLA Ops:
  0.6 75.0 %copy-start = (bf16[512,1024]{1,0:T(8,128)(2,1)S(1)}, bf16[512,1024]{1,0:T(8,128)(2,1)}, u32[]{:S(2)}) copy-start(bf16[512,1024]{1,0:T(8,128)(2,1)} %param.25) | copy-start | bytes 3145732
  0.7 15.1 %copy-start.2 = (s32[64]{0:T(128)S(1)}, s32[64]{0:T(128)}, u32[]{:S(2)}) copy-start(s32[64]{0:T(128)} %block_map.1) | copy-start | bytes 772
  9.3 10.5 %collective-permute-start = (bf16[56,128]{1,0:T(8,128)(2,1)S(1)}, bf16[56,128]{1,0:T(8,128)(2,1)S(1)}, u32[]{:S(2)}, u32[]{:S(2)}) collective-permute-start(bf16[56,128]{1,0:T(8,128)(2,1)S(1)} %bitcast.169), channel_id=1, source_target_pairs={{0,1},{1,0},{2,3},{3,2},{4,5},{5,4},{6,7},{7,6},{8,9},{9,8},{10,11... | collective-permute-start | bytes 43016 | tf_op jit(solution)/shard_map/ppermute | solution.py:56
  13.9 6.0 %collective-permute-start.1 = (bf16[16,1792]{1,0:T(8,128)(2,1)S(1)}, bf16[16,1792]{1,0:T(8,128)(2,1)S(1)}, u32[]{:S(2)}, u32[]{:S(2)}) collective-permute-start(bf16[16,1792]{1,0:T(8,128)(2,1)S(1)} %pad_maximum_fusion.4), channel_id=1, source_target_pairs={{0,1},{1,0},{2,3},{3,2},{4,5},{5,4},{6,7},{7,6},{8,9},{9,8},{10,11... | collective-permute-start | bytes 172040 | tf_op jit(solution)/shard_map/ppermute | solution.py:56
  19.1 25.1 %copy-start.19 = (bf16[1,128,1024]{2,1,0:T(8,128)(2,1)S(1)}, bf16[1,128,1024]{2,1,0:T(8,128)(2,1)}, u32[]{:S(2)}) copy-start(bf16[1,128,1024]{2,1,0:T(8,128)(2,1)} %param.16) | copy-start | bytes 786436
  20.0 25.4 %copy-start.23 = (bf16[2,7168]{1,0:T(2,128)(2,1)}, bf16[2,7168]{1,0:T(2,128)(2,1)S(1)}, u32[]{:S(2)}) copy-start(bf16[2,7168]{1,0:T(2,128)(2,1)S(1)} %broadcast_select_fusion) | copy-start | bytes 86020
  21.0 23.3 %all-to-all-start.1 = ((bf16[16,16,1792]{2,1,0:T(8,128)(2,1)}), bf16[16,16,1792]{2,1,0:T(8,128)(2,1)S(1)}, u32[]{:S(2)}, u32[]{:S(2)}) async-start(bf16[16,16,1792]{2,1,0:T(8,128)(2,1)} %broadcast_in_dim.54), calls=%async_computation.1 | async-start | bytes 1835008 | tf_op jit(solution)/shard_map/all_to_all | solution.py:52
  45.3 17.3 %all-to-all-start = ((bf16[4,128,1024]{2,1,0:T(8,128)(2,1)}), bf16[4,128,1024]{2,1,0:T(8,128)(2,1)S(1)}, u32[]{:S(2)}, u32[]{:S(2)}) async-start(bf16[4,128,1024]{2,1,0:T(8,128)(2,1)} %broadcast_in_dim.52), calls=%async_computation | async-start | bytes 2097152 | tf_op jit(solution)/shard_map/all_to_all | solution.py:52
  49.6 13.0 %collective-permute-start.2 = (bf16[256,1792]{1,0:T(8,128)(2,1)S(1)}, bf16[256,1792]{1,0:T(8,128)(2,1)}, u32[]{:S(2)}, u32[]{:S(2)}) collective-permute-start(bf16[256,1792]{1,0:T(8,128)(2,1)S(1)} %bitcast.154), channel_id=1, source_target_pairs={{0,2},{2,0},{1,3},{3,1},{4,6},{6,4},{5,7},{7,5},{8,10},{10,8},{9,1... | collective-permute-start | bytes 2752520 | tf_op jit(solution)/shard_map/ppermute | solution.py:56
  71.2 22.3 %copy-start.21 = (bf16[1,128,1024]{2,1,0:T(8,128)(2,1)S(1)}, bf16[1,128,1024]{2,1,0:T(8,128)(2,1)}, u32[]{:S(2)}) copy-start(bf16[1,128,1024]{2,1,0:T(8,128)(2,1)} %param.31) | copy-start | bytes 786436
  71.2 22.3 %all-to-all-start.2 = ((bf16[16,320,128]{2,1,0:T(8,128)(2,1)}), bf16[16,320,128]{2,1,0:T(8,128)(2,1)}, u32[]{:S(2)}, u32[]{:S(2)}) async-start(bf16[16,320,128]{2,1,0:T(8,128)(2,1)} %copy-done.4), calls=%async_computation.2 | async-start | bytes 2621440 | tf_op jit(solution)/shard_map/all_to_all | solution.py:486
  75.7 23.3 %copy-start.27 = (f32[1,4,2,128]{3,2,1,0:T(2,128)S(1)}, f32[1,4,2,128]{3,2,1,0:T(2,128)}, u32[]{:S(2)}) copy-start(f32[1,4,2,128]{3,2,1,0:T(2,128)} %get-tuple-element.82) | copy-start | bytes 12292
  75.7 23.3 %copy-start.26 = (f32[1,4,2,128]{3,2,1,0:T(2,128)S(1)}, f32[1,4,2,128]{3,2,1,0:T(2,128)}, u32[]{:S(2)}) copy-start(f32[1,4,2,128]{3,2,1,0:T(2,128)} %get-tuple-element.81) | copy-start | bytes 12292
  75.7 23.3 %copy-start.29 = (s32[2,2]{1,0:T(2,128)S(1)}, s32[2,2]{1,0:T(2,128)}, u32[]{:S(2)}) copy-start(s32[2,2]{1,0:T(2,128)} %copy-done.28) | copy-start | bytes 52
  94.6 15.3 %all-to-all-start.3 = ((bf16[4,128,1024]{2,1,0:T(8,128)(2,1)}), bf16[4,128,1024]{2,1,0:T(8,128)(2,1)S(1)}, u32[]{:S(2)}, u32[]{:S(2)}) async-start(bf16[4,128,1024]{2,1,0:T(8,128)(2,1)} %broadcast_in_dim.58), calls=%async_computation.3 | async-start | bytes 2097152 | tf_op jit(solution)/shard_map/all_to_all | solution.py:52
  98.2 29.4 %collective-permute-start.3 = (bf16[16,320,128]{2,1,0:T(8,128)(2,1)}, bf16[16,320,128]{2,1,0:T(8,128)(2,1)}, u32[]{:S(2)}, u32[]{:S(2)}) collective-permute-start(bf16[16,320,128]{2,1,0:T(8,128)(2,1)} %all-to-all-done.2.own), channel_id=1, source_target_pairs={{0,2},{2,0},{1,3},{3,1},{4,6},{6,4},{5,7},{7,5},{8,10},{10,8},{9,1... | collective-permute-start | bytes 3932168 | tf_op jit(solution)/shard_map/ppermute | solution.py:56
  111.5 14.5 %all-to-all-start.4 = ((bf16[16,64,128]{2,1,0:T(8,128)(2,1)}), bf16[16,64,128]{2,1,0:T(8,128)(2,1)S(1)}, u32[]{:S(2)}, u32[]{:S(2)}) async-start(bf16[16,64,128]{2,1,0:T(8,128)(2,1)} %shard_map.264), calls=%async_computation.4 | async-start | bytes 524288 | tf_op jit(solution)/shard_map/all_to_all | solution.py:493
  126.0 1.5 collective-permute-start.4
  127.6 84.3 %copy-start.17 = (bf16[2,512,1792]{2,1,0:T(8,128)(2,1)S(1)}, bf16[2,512,1792]{2,1,0:T(8,128)(2,1)}, u32[]{:S(2)}) copy-start(bf16[2,512,1792]{2,1,0:T(8,128)(2,1)} %copy-done.16) | copy-start | bytes 11010052
  210.7 10.5 %collective-permute-start.5 = (bf16[16,320,128]{2,1,0:T(8,128)(2,1)S(1)}, bf16[16,320,128]{2,1,0:T(8,128)(2,1)S(1)}, u32[]{:S(2)}, u32[]{:S(2)}) collective-permute-start(bf16[16,320,128]{2,1,0:T(8,128)(2,1)S(1)} %get-tuple-element.30), channel_id=1, source_target_pairs={{0,2},{2,0},{1,3},{3,1},{4,6},{6,4},{5,7},{7,5},{8,10},{10,8},{9,1... | collective-permute-start | bytes 3932168 | tf_op jit(solution)/shard_map/ppermute | solution.py:56
  220.8 6.3 %collective-permute-start.10 = (bf16[16,512,128]{2,1,0:T(8,128)(2,1)}, bf16[16,512,128]{2,1,0:T(8,128)(2,1)}, u32[]{:S(2)}, u32[]{:S(2)}) collective-permute-start(bf16[16,512,128]{2,1,0:T(8,128)(2,1)} %get-tuple-element.37), channel_id=1, source_target_pairs={{0,2},{2,0},{1,3},{3,1},{4,6},{6,4},{5,7},{7,5},{8,10},{10,8},{9,1... | collective-permute-start | bytes 6291464 | tf_op jit(solution)/shard_map/ppermute | solution.py:56
  222.7 29.3 %all-to-all-start.5 = ((bf16[16,384,128]{2,1,0:T(8,128)(2,1)}), bf16[16,384,128]{2,1,0:T(8,128)(2,1)}, u32[]{:S(2)}, u32[]{:S(2)}) async-start(bf16[16,384,128]{2,1,0:T(8,128)(2,1)} %pad_maximum_fusion.1), calls=%async_computation.5 | async-start | bytes 3145728 | tf_op jit(solution)/shard_map/all_to_all | solution.py:555
  252.0 33.5 %all-to-all-start.12 = ((bf16[16,512,128]{2,1,0:T(8,128)(2,1)}), bf16[16,512,128]{2,1,0:T(8,128)(2,1)}, u32[]{:S(2)}, u32[]{:S(2)}) async-start(bf16[16,512,128]{2,1,0:T(8,128)(2,1)} %add.387), calls=%async_computation.12 | async-start | bytes 4194304 | tf_op jit(solution)/shard_map/all_to_all | solution.py:520
  262.3 33.8 %collective-permute-start.7 = (bf16[16,256,128]{2,1,0:T(8,128)(2,1)}, bf16[16,256,128]{2,1,0:T(8,128)(2,1)}, u32[]{:S(2)}, u32[]{:S(2)}) collective-permute-start(bf16[16,256,128]{2,1,0:T(8,128)(2,1)} %get-tuple-element.35), channel_id=1, source_target_pairs={{0,2},{2,0},{1,3},{3,1},{4,6},{6,4},{5,7},{7,5},{8,10},{10,8},{9,1... | collective-permute-start | bytes 3145736 | tf_op jit(solution)/shard_map/ppermute | solution.py:56
  288.7 9.9 %all-to-all-start.13 = ((bf16[4,128,128]{2,1,0:T(8,128)(2,1)}), bf16[4,128,128]{2,1,0:T(8,128)(2,1)S(1)}, u32[]{:S(2)}, u32[]{:S(2)}) async-start(bf16[4,128,128]{2,1,0:T(8,128)(2,1)} %bitcast.41), calls=%async_computation.13 | async-start | bytes 262144 | tf_op jit(solution)/shard_map/all_to_all | solution.py:524
  292.0 4.1 copy-start.6
  298.6 18.7 %all-to-all-start.9 = ((bf16[16,256,128]{2,1,0:T(8,128)(2,1)}), bf16[16,256,128]{2,1,0:T(8,128)(2,1)}, u32[]{:S(2)}, u32[]{:S(2)}) async-start(bf16[16,256,128]{2,1,0:T(8,128)(2,1)} %add.385), calls=%async_computation.9 | async-start | bytes 2097152 | tf_op jit(solution)/shard_map/all_to_all | solution.py:520
  311.2 10.6 %copy-start.24 = (bf16[256,128]{1,0:T(8,128)(2,1)S(1)}, bf16[256,128]{1,0:T(8,128)(2,1)}, u32[]{:S(2)}) copy-start(bf16[256,128]{1,0:T(8,128)(2,1)} %get-tuple-element.70) | copy-start | bytes 196612
  311.2 31.7 %copy-start.22 = (bf16[1,256,128]{2,1,0:T(8,128)(2,1)S(1)}, bf16[1,256,128]{2,1,0:T(8,128)(2,1)}, u32[]{:S(2)}) copy-start(bf16[1,256,128]{2,1,0:T(8,128)(2,1)} %get-tuple-element.69) | copy-start | bytes 196612
  317.3 27.0 %all-to-all-start.6 = ((bf16[4,256,1024]{2,1,0:T(8,128)(2,1)}), bf16[4,256,1024]{2,1,0:T(8,128)(2,1)S(1)}, u32[]{:S(2)}, u32[]{:S(2)}) async-start(bf16[4,256,1024]{2,1,0:T(8,128)(2,1)} %pad_maximum_fusion), calls=%async_computation.6 | async-start | bytes 4194304 | tf_op jit(solution)/shard_map/all_to_all | solution.py:590
  321.8 21.1 %collective-permute-start.11 = (bf16[256,128]{1,0:T(8,128)(2,1)S(1)}, bf16[256,128]{1,0:T(8,128)(2,1)S(1)}, u32[]{:S(2)}, u32[]{:S(2)}) collective-permute-start(bf16[256,128]{1,0:T(8,128)(2,1)S(1)} %copy-done.24), channel_id=1, source_target_pairs={{0,4},{4,0},{1,5},{5,1},{2,6},{6,2},{3,7},{7,3},{8,12},{12,8},{9,1... | collective-permute-start | bytes 196616 | tf_op jit(solution)/shard_map/ppermute | solution.py:56
  344.9 9.7 %all-to-all-start.10 = ((bf16[4,96,128]{2,1,0:T(8,128)(2,1)}), bf16[4,96,128]{2,1,0:T(8,128)(2,1)S(1)}, u32[]{:S(2)}, u32[]{:S(2)}) async-start(bf16[4,96,128]{2,1,0:T(8,128)(2,1)} %bitcast.28), calls=%async_computation.10 | async-start | bytes 196608 | tf_op jit(solution)/shard_map/all_to_all | solution.py:577
  357.5 6.5 %copy-start.20 = (bf16[1,128,1024]{2,1,0:T(8,128)(2,1)S(1)}, bf16[1,128,1024]{2,1,0:T(8,128)(2,1)}, u32[]{:S(2)}) copy-start(bf16[1,128,1024]{2,1,0:T(8,128)(2,1)} %param.16) | copy-start | bytes 786436
  357.5 55.0 %all-to-all-start.14 = ((bf16[16,1024,128]{2,1,0:T(8,128)(2,1)}), bf16[16,1024,128]{2,1,0:T(8,128)(2,1)}, u32[]{:S(2)}, u32[]{:S(2)}) async-start(bf16[16,1024,128]{2,1,0:T(8,128)(2,1)} %broadcast_in_dim.117), calls=%async_computation.14 | async-start | bytes 8388608 | tf_op jit(solution)/shard_map/all_to_all | solution.py:52
  364.1 3.8 collective-permute-start.8
  414.2 8.4 %copy-start.35 = (f32[1024]{0:T(1024)S(1)}, f32[1024]{0:T(1024)}, u32[]{:S(2)}) copy-start(f32[1024]{0:T(1024)} %get-tuple-element.63) | copy-start | bytes 12292
  414.2 8.4 %copy-start.34 = (f32[1024]{0:T(1024)S(1)}, f32[1024]{0:T(1024)}, u32[]{:S(2)}) copy-start(f32[1024]{0:T(1024)} %get-tuple-element.64) | copy-start | bytes 12292
  414.2 8.5 %copy-start.33 = (f32[1024]{0:T(1024)S(1)}, f32[1024]{0:T(1024)}, u32[]{:S(2)}) copy-start(f32[1024]{0:T(1024)} %get-tuple-element.39) | copy-start | bytes 12292
  414.2 8.5 %copy-start.32 = (f32[1024]{0:T(1024)S(1)}, f32[1024]{0:T(1024)}, u32[]{:S(2)}) copy-start(f32[1024]{0:T(1024)} %get-tuple-element.38) | copy-start | bytes 12292
  414.2 8.5 %copy-start.8 = (bf16[512,768]{1,0:T(8,128)(2,1)S(1)}, bf16[512,768]{1,0:T(8,128)(2,1)}, u32[]{:S(2)}) copy-start(bf16[512,768]{1,0:T(8,128)(2,1)} %copy-done.7) | copy-start | bytes 2359300
  414.2 35.8 %all-to-all-start.11 = ((bf16[16,512,128]{2,1,0:T(8,128)(2,1)}), bf16[16,512,128]{2,1,0:T(8,128)(2,1)}, u32[]{:S(2)}, u32[]{:S(2)}) async-start(bf16[16,512,128]{2,1,0:T(8,128)(2,1)} %broadcast_in_dim.114), calls=%async_computation.11 | async-start | bytes 4194304 | tf_op jit(solution)/shard_map/all_to_all | solution.py:52
  421.8 87.9 %collective-permute-start.12 = (bf16[16,1024,128]{2,1,0:T(8,128)(2,1)}, bf16[16,1024,128]{2,1,0:T(8,128)(2,1)}, u32[]{:S(2)}, u32[]{:S(2)}) collective-permute-start(bf16[16,1024,128]{2,1,0:T(8,128)(2,1)} %all-to-all-done.14), channel_id=1, source_target_pairs={{0,2},{2,0},{1,3},{3,1},{4,6},{6,4},{5,7},{7,5},{8,10},{10,8},{9,1... | collective-permute-start | bytes 12582920 | tf_op jit(solution)/shard_map/ppermute | solution.py:56
  423.2 28.9 %copy-start.31 = (f32[1024]{0:T(1024)S(1)}, f32[1024]{0:T(1024)}, u32[]{:S(2)}) copy-start(f32[1024]{0:T(1024)} %get-tuple-element.87) | copy-start | bytes 12292
  450.0 40.0 %collective-permute-start.9 = (bf16[16,512,128]{2,1,0:T(8,128)(2,1)}, bf16[16,512,128]{2,1,0:T(8,128)(2,1)}, u32[]{:S(2)}, u32[]{:S(2)}) collective-permute-start(bf16[16,512,128]{2,1,0:T(8,128)(2,1)} %all-to-all-done.11), channel_id=1, source_target_pairs={{0,2},{2,0},{1,3},{3,1},{4,6},{6,4},{5,7},{7,5},{8,10},{10,8},{9,1... | collective-permute-start | bytes 6291464 | tf_op jit(solution)/shard_map/ppermute | solution.py:56
  452.1 2.1 collective-permute-start.6
  469.7 9.4 %all-to-all-start.8 = ((f32[4,56,128]{2,1,0:T(8,128)}), f32[4,56,128]{2,1,0:T(8,128)S(1)}, u32[]{:S(2)}, u32[]{:S(2)}) async-start(f32[4,56,128]{2,1,0:T(8,128)} %broadcast_in_dim.63), calls=%async_computation.8 | async-start | bytes 229376 | tf_op jit(solution)/shard_map/all_to_all | solution.py:52
  479.8 52.0 %copy-start.30 = (f32[1,512]{1,0:T(1,128)}, f32[1,512]{1,0:T(1,128)S(1)}, u32[]{:S(2)}) copy-start(f32[1,512]{1,0:T(1,128)S(1)} %get-tuple-element.73) | copy-start | bytes 6148
  520.1 12.2 %copy-start.1 = (bf16[512,1024]{1,0:T(8,128)(2,1)S(1)}, bf16[512,1024]{1,0:T(8,128)(2,1)}, u32[]{:S(2)}) copy-start(bf16[512,1024]{1,0:T(8,128)(2,1)} %param.25) | copy-start | bytes 3145732
  (17 other events, 36.8 us)

commit v2 on v1

v2 whole, which is shorter than its diff:
```python
import functools
import math

import jax
import jax.numpy as jnp
from jax import lax
from jax.experimental import pallas as pl
from jax.experimental.pallas import tpu as pltpu
from jax.sharding import Mesh
from jax.sharding import PartitionSpec as P

ROT = 16
EPS = 1e-05
NEG_FILL = -1e30
BF = jnp.bfloat16
F32 = jnp.float32
RING = ("xh", "xl")
PLANE = ("y", "z")
MIB = 1 << 20

NN = (((1,), (0,)), ((), ()))
NT = (((1,), (1,)), ((), ()))
TN = (((0,), (0,)), ((), ()))


def mm(left, right, dims=NN):
    return lax.dot_general(left, right, dims, preferred_element_type=F32)


def mult(value, step):
    return pl.multiple_of(value, step)


def whole(space=pltpu.VMEM):
    return pl.BlockSpec(memory_space=space)


def call(body, outs, ins, scratch=(), flops=0, moved=0, limit=48):
    return pl.pallas_call(
        body,
        out_shape=outs,
        in_specs=ins,
        out_specs=[whole() for _ in outs],
        scratch_shapes=list(scratch),
        cost_estimate=pl.CostEstimate(flops=flops, bytes_accessed=moved, transcendentals=0),
        compiler_params=pltpu.CompilerParams(vmem_limit_bytes=limit * MIB),
    )


def to_all(array_in, axes, count):
    copies = jnp.broadcast_to(array_in[None], (count,) + array_in.shape)
    return lax.all_to_all(copies, axes, 0, 0, tiled=True)


def swap(array_in, axis):
    return lax.ppermute(array_in, axis, [(0, 1), (1, 0)])


def shift_ring(array_in, places):
    spots = [(x % 2) * 2 + x // 2 for x in range(4)]
    return lax.ppermute(
        array_in, ("xl", "xh"), [(spots[x], spots[(x + places) % 4]) for x in range(4)]
    )


def in_order(first, mine, other):
    return jnp.where(first, jnp.stack([mine, other]), jnp.stack([other, mine]))


def turn(tile, cosine, sine_low, sine_high):
    return (
        tile * cosine
        + pltpu.roll(tile, 120, 1) * sine_low
        + pltpu.roll(tile, 8, 1) * sine_high
    )


def sine_parts(sine, sign):
    spot = lax.broadcasted_iota(jnp.int32, sine.shape, 1) % 64
    low = jnp.where(spot < 8, -sign * sine, 0.0)
    high = jnp.where((spot >= 8) & (spot < 16), sign * sine, 0.0)
    return low, high


def project_kernel(
    place, rows0, rows1, rows2, rows3, gain, shift, mlp_gain, mlp_shift, weight_own, weight_other,
    bias, out_weight, cosine, sine, send, normed, normed_mlp, xhat, upstream,
):
    chip, half_in = place[1], place[2]
    here = pl.ds(mult(half_in * 512, 512), 512)
    there = pl.ds(mult(512 - half_in * 512, 512), 512)
    left = lax.broadcasted_iota(jnp.int32, (64, 128), 1) < 64
    left_all = lax.broadcasted_iota(jnp.int32, (128, 128), 1) < 64

    def pack(tile):
        low, high = tile[:64], tile[64:]
        return (
            jnp.where(left, low, pltpu.roll(high, 64, 1)).astype(BF),
            jnp.where(left, pltpu.roll(low, 64, 1), high).astype(BF),
        )

    for back, source in enumerate((rows0, rows1, rows2, rows3)):
        origin = (chip + 4 - back) % 4
        stream, half_x = origin // 2, origin % 2
        rows = pl.ds(back * 128, 128)
        moved = source[0].astype(F32)
        moved = moved - jnp.mean(moved, axis=1, keepdims=True)
        spread = jnp.mean(moved * moved, axis=1, keepdims=True)
        unit = moved * lax.rsqrt(spread + EPS)
        xhat[rows, :] = unit.astype(BF)
        normed[rows, :] = (unit * gain[...] + shift[...]).astype(BF)
        normed_mlp[rows, :] = (unit * mlp_gain[...] + mlp_shift[...]).astype(BF)
        upstream[rows, :] = source[1]
        project = (
            mm(normed[rows, here], weight_own[...]) + mm(normed[rows, there], weight_other[...]) + bias[...]
        )
        grads = mm(source[1], out_weight[...], NT)
        cos = cosine[rows, :]
        low, high = sine_parts(sine[rows, :], 1.0)
        for pair in range(2):
            at = pair * 128
            query = pack(turn(project[:, at : at + 128], cos, low, high) * 0.125)
            grad = pack(grads[:, at : at + 128])
            key = turn(project[:, 256 + at : 384 + at], cos, low, high)
            value = project[:, 512 + at : 640 + at]
            key_value = (
                jnp.where(left_all, key, pltpu.roll(value, 64, 1)).astype(BF),
                jnp.where(left_all, pltpu.roll(key, 64, 1), value).astype(BF),
            )
            for member in range(2):
                for half in range(2):
                    target = stream * 8 + (pair * 2 + member) * 2 + half
                    send[target, pl.ds(mult(half_x * 128, 128), 128), :] = key_value[member]
                    for core in range(2):
                        quarter = half * 2 + core
                        cut = slice(quarter * 16, quarter * 16 + 16)
                        spot = core * 32 + half_x * 16
                        send[target, pl.ds(mult(256 + spot, 16), 16), :] = query[member][cut]
                        send[target, pl.ds(mult(320 + spot, 16), 16), :] = grad[member][cut]


ROWS = 256
KEYS = 1024
SPAN = ROWS * 4
TILES = 8192 // SPAN
DIAGONAL = SPAN // KEYS


def attend_kernel(
    place, block_map, own, other, out_own, out_other,
    kv, kv_turned, q_grad, scores, chances, key_sums, rows_out,
):
    core, quarter, second, third = place[0], place[1], place[2], place[3]
    left16 = lax.broadcasted_iota(jnp.int32, (16, 128), 1) < 64
    left = lax.broadcasted_iota(jnp.int32, (ROWS, 128), 1) < 64
    def fill(source, from_core):
        @pl.loop(0, 32)
        def _(i):
            group, half_x = i // 2, i % 2
            block = block_map[i * 2 + from_core]
            mirror = 127 - block
            kv[pl.ds(mult(block * 64, 64), 64), :] = source[group, pl.ds(mult(half_x * 128, 64), 64), :]
            kv[pl.ds(mult(mirror * 64, 64), 64), :] = source[group, pl.ds(mult(half_x * 128 + 64, 64), 64), :]
            spot = core * 32 + half_x * 16
            query = source[group, pl.ds(mult(256 + spot, 16), 16), :].astype(F32)
            grad = source[group, pl.ds(mult(320 + spot, 16), 16), :].astype(F32)
            q_grad[pl.ds(mult(block * 16, 16), 16), :] = jnp.where(left16, query, pltpu.roll(grad, 64, 1)).astype(BF)
            q_grad[pl.ds(mult(mirror * 16, 16), 16), :] = jnp.where(left16, pltpu.roll(query, 64, 1), grad).astype(BF)
    fill(own, core)
    fill(other, 1 - core)
    @pl.loop(0, 16)
    def _(c):
        for d in range(4):
            cut = pl.ds(mult(c * 512 + d*128, 128), 128)
            kv_turned[:, cut] = kv[cut, :].astype(F32).T.astype(BF)
            key_sums[:, cut] = jnp.zeros((128, 128), F32)
    row = lax.broadcasted_iota(jnp.int32, (ROWS, 1), 0)
    offset = (row // 16) * 64 + quarter * 16 + row % 16
    spots = lax.broadcasted_iota(jnp.int32, (ROWS, KEYS), 1)
    def start_of(position):
        return jnp.where(position >= third, third, jnp.where(position >= second, second, 0))
    @pl.loop(0, TILES)
    def _(step):
        tile = TILES-1 - step
        rows = pl.ds(mult(tile * ROWS, ROWS), ROWS)
        base = tile * SPAN
        both = q_grad[rows, :]
        query, grad = both[:, :64], both[:, 64:]
        position = base + offset
        first = start_of(position)
        diag = tile * DIAGONAL
        low = start_of(base + quarter * 16) // KEYS
        high = (start_of(base + SPAN - 64 + quarter * 16 + 15) + KEYS - 1) // KEYS
        high = jnp.minimum(jnp.maximum(high, low), diag)
        low_ = jnp.minimum(low, diag)
        def cut_of(j):
            return pl.ds(mult(j * KEYS, KEYS), KEYS)
        def fold(top, part):
            for c in range(KEYS // 128):
                top = jnp.maximum(top, part[:, c * 128 : c * 128 + 128])
            return top
        def plain(j, top):
            part = mm(query, kv_turned[0:64, cut_of(j)])
            scores[:, cut_of(j)] = part
            return fold(top, part)
        def masked(j, top):
            part = mm(query, kv_turned[0:64, cut_of(j)])
            key_at = spots + j * KEYS
            part = jnp.where((key_at <= position) & (key_at >= first), part, NEG_FILL)
            scores[:, cut_of(j)] = part
            return fold(top, part)
        top = jnp.full((ROWS, 128), NEG_FILL, F32)
        top = lax.fori_loop(low_, high, masked, top)
        top = lax.fori_loop(high, diag, plain, top)
        for d in range(DIAGONAL):
            top = masked(diag + d, top)
        row_top = jnp.max(top, axis=1, keepdims=True)
        def weigh(j, state):
            total, mixed = state
            part = jnp.exp(scores[:, cut_of(j)] - row_top)
            for c in range(KEYS // 128):
                total = total + part[:, c * 128 : c * 128 + 128]
            rounded = part.astype(BF)
            chances[:, cut_of(j)] = rounded
            return total, mixed + mm(rounded, kv[cut_of(j), :])
        zero = jnp.zeros((ROWS, 128), F32)
        total, mixed = lax.fori_loop(low_, diag + DIAGONAL, weigh, (zero, zero))
        share = 1.0 / jnp.sum(total, axis=1, keepdims=True)
        mixed = mixed * share
        scaled = jnp.where(left, both.astype(F32), both.astype(F32) * share)
        delta = jnp.sum(jnp.where(left, 0.0, scaled * mixed), axis=1, keepdims=True)
        grad_scaled = scaled[:, 64:].astype(BF)
        turned = scaled.T.astype(BF)
        query_turned, grad_turned = turned[:64], turned[64:]
        def back(j, query_sum):
            cut = cut_of(j)
            part = chances[:, cut]
            along = mm(grad_scaled, kv_turned[64:128, cut])
            score_grad = (part.astype(F32) * (along - delta)).astype(BF)
            key_sums[0:64, cut] += mm(query_turned, score_grad)
            key_sums[64:128, cut] += mm(grad_turned, part)
            return query_sum + mm(score_grad, kv[cut, :])
        query_sum = lax.fori_loop(low_, diag + DIAGONAL, back, zero)
        rows_out[rows, :] = jnp.where(left, query_sum * 0.125, mixed).astype(BF)
    @pl.loop(0, 16)
    def _(c):
        for d in range(4):
            cut = pl.ds(mult(c * 512+d*128, 128), 128)
            kv[cut, :] = key_sums[:, cut].T.astype(BF)
    def spill(target, to_core):
        @pl.loop(0, 32)
        def _(i):
            group, half_x = i // 2, i % 2
            block = block_map[i * 2 + to_core]
            mirror = 127 - block
            target[group, pl.ds(mult(half_x * 128, 64), 64), :] = kv[pl.ds(mult(block * 64, 64), 64), :]
            target[group, pl.ds(mult(half_x * 128 + 64, 64), 64), :] = kv[pl.ds(mult(mirror * 64, 64), 64), :]
            spot = 256 + half_x * 32
            target[group, pl.ds(mult(spot, 16), 16), :] = rows_out[pl.ds(mult(block * 16, 16), 16), :]
            target[group, pl.ds(mult(spot + 16, 16), 16), :] = rows_out[pl.ds(mult(mirror * 16, 16), 16), :]
    spill(out_own, core)
    spill(out_other, 1 - core)


def return_kernel(
    place, back, cosine, sine, normed, xhat, upstream, weight, early,
    out_own, out_other, normed_grad, project_grad, mixed_out, heads, small,
):
    core, chip = place[0], place[1]
    left = lax.broadcasted_iota(jnp.int32, (128, 128), 1) < 64
    for behind in range(4):
        origin = (chip + 4 - behind) % 4
        stream, half_x = origin // 2, origin % 2
        rows = pl.ds(behind * 128, 128)
        cos = cosine[rows, :]
        low, high = sine_parts(sine[rows, :], -1.0)
        for pair in range(2):
            pieces = []
            for member in range(2):
                base = stream * 8 + (pair * 2 + member) * 2
                cut = pl.ds(mult(half_x * 128, 128), 128)
                key_value = back[base, cut, :].astype(F32) + back[base + 1, cut, :].astype(F32)
                for upper in range(2):
                    for half in range(2):
                        for of_core in range(2):
                            flipped = of_core ^ core
                            spot = 256 + flipped * 64 + (half_x * 2 + upper) * 16
                            heads[
                                member, pl.ds(upper * 64 + (half * 2 + of_core) * 16, 16), :
                            ] = back[base + half, pl.ds(mult(spot, 16), 16), :]
                pieces.append((heads[member].astype(F32), key_value))
            (row0, kv0), (row1, kv1) = pieces
            at = pair * 128
            query = jnp.where(left, row0, pltpu.roll(row1, 64, 1))
            key = jnp.where(left, kv0, pltpu.roll(kv1, 64, 1))
            value = jnp.where(left, pltpu.roll(kv0, 64, 1), kv1)
            mixed = jnp.where(left, pltpu.roll(row0, 64, 1), row1)
            project_grad[rows, at : at + 128] = turn(query, cos, low, high).astype(BF)
            project_grad[rows, 256 + at : 384 + at] = turn(key, cos, low, high).astype(BF)
            project_grad[rows, 512 + at : 640 + at] = value.astype(BF)
            mixed_out[rows, at : at + 128] = mixed.astype(BF)

    small[...] = jnp.zeros_like(small)
    for k in range(32):
        small[0, k // 2, k % 2 : k % 2 + 1, :] = early[k : k + 1, :]

    def keep(first, sums):
        for n in range(sums.shape[1] // 128):
            k = first + n
            small[1, k // 2, k % 2 : k % 2 + 1, :] = sums[:, n * 128 : n * 128 + 128]

    gain_sums = jnp.zeros((1, 1024), F32)
    shift_sums = jnp.zeros((1, 1024), F32)
    bias_sums = jnp.zeros((1, 768), F32)
    for block in range(4):
        rows = pl.ds(block * 128, 128)
        grads = project_grad[rows, :]
        entry = mm(grads, weight[...], NT)
        normed_grad[rows, :] = entry
        gain_sums += jnp.sum(entry * xhat[rows, :].astype(F32), axis=0, keepdims=True)
        shift_sums += jnp.sum(entry, axis=0, keepdims=True)
        bias_sums += jnp.sum(grads.astype(F32), axis=0, keepdims=True)
    keep(0, gain_sums)
    keep(8, shift_sums)
    keep(16, bias_sums)

    for flip, target in ((0, out_own), (1, out_other)):
        to_core = core ^ flip
        for part in range(2):
            columns = normed[:, pl.ds(mult(part * 512 + to_core * 256, 256), 256)]
            for block in range(3):
                grads = mm(columns, project_grad[:, block * 256 : block * 256 + 256], TN).astype(BF)
                for n in range(2):
                    slot = part * 6 + block * 2 + n
                    target[:, slot * 16 : slot * 16 + 16, :] = grads[:, n * 128 : n * 128 + 128].reshape(
                        16, 16, 128
                    )
        for block in range(2):
            columns = upstream[:, pl.ds(mult(to_core * 512 + block * 256, 256), 256)]
            grads = mm(mixed_out[...], columns, TN).astype(BF)
            for n in range(2):
                at = 192 + (block * 2 + n) * 16
                target[:, at : at + 16, :] = grads[:, n * 128 : n * 128 + 128].reshape(16, 16, 128)
        target[:, 256:272, :] = small[to_core].astype(BF)


def feed_weights_kernel(place, normed, inner_grad, active, upstream, out_own, out_other):
    for flip, target in ((0, out_own), (1, out_other)):
        core = place[0] ^ flip
        for part in range(2):
            rows = normed[:, pl.ds(mult(part * 512 + core * 256, 256), 256)]
            for quad in range(4):
                grads = mm(rows, inner_grad[:, quad * 256 : quad * 256 + 256], TN).astype(BF)
                for n in range(2):
                    slot = part * 8 + quad * 2 + n
                    target[:, slot * 16 : slot * 16 + 16, :] = grads[:, n * 128 : n * 128 + 128].reshape(
                        16, 16, 128
                    )
        rows = active[:, pl.ds(mult(core * 512, 512), 512)]
        for quad in range(4):
            grads = mm(rows, upstream[:, quad * 256 : quad * 256 + 256], TN).astype(BF)
            for n in range(2):
                at = 256 + (quad * 2 + n) * 32
                target[:, at : at + 32, :] = grads[:, n * 128 : n * 128 + 128].reshape(16, 32, 128)


def spread_kernel(place, piece, out, *, columns):
    for behind, slot, rows, step, at in columns:
        start = at
        if step:
            start = mult(at + ((place[1] + 4 - behind) % 4) * step, 128)
        out[:, pl.ds(start, 128)] = piece[0, slot : slot + rows, :].astype(F32)


def spread(place, pieces, shape_out, block, at_row, grid, in_map, out_map, columns):
    height, width = block
    return pl.pallas_call(
        functools.partial(spread_kernel, columns=columns),
        out_shape=jax.ShapeDtypeStruct(shape_out, F32),
        grid_spec=pltpu.PrefetchScalarGridSpec(
            num_scalar_prefetch=1,
            grid=grid,
            in_specs=[pl.BlockSpec((1, at_row, 128), in_map)],
            out_specs=pl.BlockSpec((height, width), out_map),
        ),
        cost_estimate=pl.CostEstimate(
            flops=0, bytes_accessed=shape_out[0] * shape_out[1] * 6, transcendentals=0
        ),
        compiler_params=pltpu.CompilerParams(vmem_limit_bytes=32 * MIB),
    )(place, pieces)


def shape(*sizes, dtype=BF):
    return jax.ShapeDtypeStruct(sizes, dtype)


def normalized(hidden):
    moved = hidden - jnp.mean(hidden, axis=-1, keepdims=True)
    spread_out = jnp.mean(moved * moved, axis=-1, keepdims=True)
    scale = lax.rsqrt(spread_out + EPS)
    return moved * scale, scale


def per_device(
    hidden_in, doc_ids, block_map, attn_gain, attn_shift, mlp_gain, mlp_shift, qkv_weight, qkv_bias,
    out_weight, out_bias, in_weight, in_bias, proj_weight, proj_bias, cotangent,
):
    y, z = lax.axis_index("y"), lax.axis_index("z")
    xh, xl = lax.axis_index("xh"), lax.axis_index("xl")
    core = lax.axis_index("core")
    group = y * 4 + z
    chip = xh * 2 + xl
    low_half = xh == 0
    smem = whole(pltpu.SMEM)
    place = jnp.stack([core, chip, xh, xl]).astype(jnp.int32)

    payload = jnp.stack([hidden_in[0], cotangent[0]])
    ring = [payload] + [shift_ring(payload, d) for d in (1, 2, 3)]
    origins = (chip + 4 - jnp.arange(4, dtype=jnp.int32)) % 4

    partner = (1 - xh) * 2 + xl

    def qkv_columns_of(which, first_row, rows):
        return jnp.concatenate(
            [lax.dynamic_slice(qkv_weight, (first_row, k * 1024 + which * 256), (rows, 256)) for k in range(3)],
            axis=1,
        )

    piece = swap(qkv_columns_of(partner, group * 32, 32), "xh")
    qkv_other = to_all(piece, PLANE, 16).reshape(512, 768)
    qkv_own = qkv_columns_of(chip, 0, 512)
    piece = swap(lax.dynamic_slice(in_weight, (core * 256, partner * 1024), (256, 1024)), "xh")
    in_other = in_order(core == 0, piece, swap(piece, "core")).reshape(512, 1024)
    in_own = lax.dynamic_slice(in_weight, (0, chip * 1024), (512, 1024))

    segment = doc_ids[0]
    bounds = jnp.stack([jnp.sum((segment < label).astype(jnp.int32)) for label in (1, 2)])
    bound_parts = jnp.stack([bounds // 128, bounds % 128]).reshape(4).astype(BF)
    vectors = jnp.concatenate(
        [attn_gain, attn_shift, mlp_gain, mlp_shift, qkv_bias, in_bias, out_bias, proj_bias,
         bound_parts, jnp.zeros((508,), BF)]
    ).reshape(56, 128)
    vectors_other = swap(vectors, "xh")
    pairs = in_order(low_half, vectors.reshape(-1), vectors_other.reshape(-1))
    a_gain = pairs[:, 0:512].reshape(1, 1024).astype(F32)
    a_shift = pairs[:, 512:1024].reshape(1, 1024).astype(F32)
    m_gain = pairs[:, 1024:1536].reshape(1, 1024).astype(F32)
    m_shift = pairs[:, 1536:2048].reshape(1, 1024).astype(F32)
    qkv_bias_all = pairs[:, 2048:3584].reshape(3, 1024).astype(F32)
    qkv_bias_here = lax.dynamic_slice(qkv_bias_all, (0, chip * 256), (3, 256)).reshape(1, 768)
    in_bias_here = lax.dynamic_slice(
        pairs[:, 3584:5632].reshape(1, 4096), (0, chip * 1024), (1, 1024)
    ).astype(F32)
    branch_bias = (
        pairs[:, 5632:6144].reshape(1, 1024).astype(F32) + pairs[:, 6144:6656].reshape(1, 1024).astype(F32)
    )
    bound_pairs = pairs[:, 6656:6660].astype(F32).astype(jnp.int32)
    doc_bounds = bound_pairs[:, 0:2] * 128 + bound_pairs[:, 2:4]

    blocks = jnp.take(block_map, (group * 2 + origins % 2) * 2 + core)[:, None]
    steps = jnp.arange(64, dtype=jnp.int32)[None]
    position = jnp.concatenate([blocks * 64 + steps, (127 - blocks) * 64 + steps], axis=1)
    row_bounds = jnp.take(doc_bounds, origins // 2, axis=0)
    second, third = row_bounds[:, 0:1], row_bounds[:, 1:2]
    first = jnp.where(position >= third, third, jnp.where(position >= second, second, 0))
    relative = (position - first).astype(F32).reshape(512, 1)
    frequency = 10000.0 ** (-(jnp.arange(0, ROT, 2).astype(F32) / ROT))
    lanes = jnp.concatenate([frequency, frequency, jnp.zeros((48,), F32)])
    angles = relative * jnp.concatenate([lanes, lanes])[None]
    cosine, sine = jnp.cos(angles), jnp.sin(angles)

    out_here = lax.dynamic_slice(out_weight, (xl * 256, 0), (256, 1024))
    send, normed, normed_mlp, xhat, upstream = call(
        project_kernel,
        [shape(16, 384, 128)] + [shape(512, 1024)] * 4,
        [smem] + [whole()] * 14,
        flops=2 * 512 * 1024 * 1024,
        moved=12 * MIB,
    )(place, *ring, a_gain, a_shift, m_gain, m_shift, qkv_own, qkv_other, qkv_bias_here, out_here,
      cosine, sine)
    heads_own = lax.all_to_all(send, PLANE, 0, 0, tiled=True)
    heads_other = swap(heads_own, "core")

    in_here = in_order(low_half, in_own, in_other).reshape(1024, 1024)
    inner = mm(normed_mlp, in_here) + in_bias_here
    bell = 0.5 * (1.0 + lax.erf(inner * (2.0**-0.5)))
    active = (inner * bell).astype(BF)
    proj_here = lax.dynamic_slice(proj_weight, (xl * 1024, 0), (1024, 1024))
    branch_mlp = mm(active, proj_here)
    active_grad = mm(upstream, proj_here, NT)
    slope = bell + inner * jnp.exp(-0.5 * inner * inner) * (1.0 / math.sqrt(2.0 * math.pi))
    inner_grad = (active_grad * slope).astype(BF)
    normed_mlp_grad = mm(inner_grad, in_here, NT)

    def column_sum(array_in):
        return jnp.sum(array_in.astype(F32), axis=0)

    early = jnp.concatenate(
        [
            column_sum(normed_mlp_grad * xhat.astype(F32)),
            column_sum(normed_mlp_grad),
            column_sum(cotangent[0]),
            column_sum(inner_grad),
        ]
    ).reshape(32, 128)
    entry_mlp = normed_mlp_grad * m_gain

    feed_own, feed_other = call(
        feed_weights_kernel,
        [shape(16, 512, 128)] * 2,
        [smem] + [whole()] * 4,
        flops=4 * 512 * 1024 * 1024,
        moved=8 * MIB,
    )(place, normed_mlp, inner_grad, active, upstream)
    feed_both = feed_own + swap(feed_other, "core")

    def reduce_plane(both):
        parts = lax.all_to_all(both, PLANE, 0, 0, tiled=True)
        return jnp.sum(parts.astype(F32), axis=0).astype(BF)

    def around(parts, rest=()):
        got = [jnp.concatenate([lax.dynamic_index_in_dim(parts, xh, 0, False), *rest])]
        for d in (1, 2, 3):
            half = ((chip + d) % 4) // 2
            got.append(
                shift_ring(jnp.concatenate([lax.dynamic_index_in_dim(parts, half, 0, False), *rest]), d)
            )
        return got

    heads_own, heads_other, feed_both, early, entry_mlp, branch_mlp = lax.optimization_barrier(
        (heads_own, heads_other, feed_both, early, entry_mlp, branch_mlp)
    )
    feed = reduce_plane(feed_both)
    quarter = (group % 2) * 2 + core
    bounds_here = lax.dynamic_index_in_dim(doc_bounds, group // 8, 0, keepdims=False)
    spot = jnp.concatenate([jnp.stack([core, quarter]).astype(jnp.int32), bounds_here])
    back_own, back_other = call(
        attend_kernel,
        [shape(16, 320, 128)] * 2,
        [smem, smem] + [whole()] * 2,
        scratch=[
            pltpu.VMEM((8192, 128), BF),
            pltpu.VMEM((128, 8192), BF),
            pltpu.VMEM((2048, 128), BF),
            pltpu.VMEM((ROWS, 8192), F32),
            pltpu.VMEM((ROWS, 8192), BF),
            pltpu.VMEM((128, 8192), F32),
            pltpu.VMEM((2048, 128), BF),
        ],
        flops=45 * 10**9,
        moved=6 * MIB,
    )(spot, block_map, heads_own, heads_other)

    arrived = swap(back_other, "core")
    returned = lax.all_to_all(
        jnp.concatenate(
            [back_own[:, :256] + arrived[:, :256], back_own[:, 256:], arrived[:, 256:]], axis=1
        ),
        PLANE, 0, 0, tiled=True,
    )

    feed, back_own = lax.optimization_barrier((feed, back_own))
    in_parts = around(feed[:256].reshape(2, 128, 128))
    feed_all = lax.all_gather(
        jnp.concatenate(in_parts + [feed[256:], swap(feed[256:], "xl")]), ("core",) + PLANE, axis=0
    )

    qkv_here = in_order(low_half, qkv_own, qkv_other).reshape(1024, 768)
    heads_grad_own, heads_grad_other, normed_grad, project_grad, mixed = call(
        return_kernel,
        [shape(16, 272, 128)] * 2 + [shape(512, 1024, dtype=F32), shape(512, 768), shape(512, 256)],
        [smem] + [whole()] * 8,
        scratch=[pltpu.VMEM((2, 128, 128), BF), pltpu.VMEM((2, 16, 16, 128), F32)],
        flops=4 * 512 * 1024 * 1024,
        moved=9 * MIB,
    )(place, returned, cosine, sine, normed, xhat, upstream, qkv_here, early)

    heads_sum = reduce_plane(heads_grad_own + swap(heads_grad_other, "core"))
    heads_parts = around(heads_sum[:192].reshape(2, 96, 128), (heads_sum[256:], heads_sum[192:256]))
    beside = jnp.where(xl == 0, heads_parts[3], heads_parts[1])
    heads_all = to_all(
        jnp.concatenate([part[:112] for part in heads_parts] + [heads_parts[0][112:], beside[112:]]),
        PLANE, 16,
    )
    heads_core = swap(heads_all, "core")

    branch = branch_mlp + mm(mixed, out_here)
    entry = normed_grad * a_gain + entry_mlp
    to_rows = jnp.concatenate([branch.reshape(4, 128, 1024), entry.reshape(4, 128, 1024)], axis=1).astype(BF)
    ring_rows = to_rows[0].astype(F32)
    for d in (1, 2, 3):
        ring_rows = ring_rows + shift_ring(to_rows[d], 4 - d).astype(F32)
    own_hidden = hidden_in[0].astype(F32)
    hidden_out = (own_hidden + ring_rows[:128] + branch_bias).astype(BF)[None]
    own_xhat, own_scale = normalized(own_hidden)
    own_entry = ring_rows[128:]
    hidden_grad = (
        cotangent[0].astype(F32)
        + own_scale
        * (
            own_entry
            - jnp.mean(own_entry, axis=1, keepdims=True)
            - own_xhat * jnp.mean(own_entry * own_xhat, axis=1, keepdims=True)
        )
    )[None]

    small = in_order(core == 0, heads_all[:, :448], heads_core[:, :448]).reshape(2, 16, 4, 112, 128)
    small = small[:, :, :, 96:98].astype(F32).transpose(2, 0, 1, 3, 4).reshape(4, 2, 4, 1024)
    common = jnp.sum(small, axis=0)
    in_order_of_chips = jnp.take(small, origins, axis=0)
    own_columns = lax.dynamic_slice(common, (0, 0, xh * 512), (2, 4, 512))
    in_bias_grad = lax.dynamic_slice(in_order_of_chips[:, 0, 3].reshape(4096), (xh * 2048,), (2048,))
    qkv_bias_grad = in_order_of_chips[:, 1, 2:].reshape(4, 2048)[:, :768].reshape(4, 3, 256)
    qkv_bias_grad = qkv_bias_grad.transpose(1, 0, 2).reshape(3072)
    qkv_bias_grad = lax.dynamic_slice(qkv_bias_grad, (xh * 1536,), (1536,))

    in_weight_grad = spread(
        place, feed_all, (512, 4096), (16, 4096), 512, (32,),
        lambda g, place: (g, 0, 0), lambda g, place: (g, 0),
        [(c, c * 128 + n * 16, 16, 1024, n * 128) for c in range(4) for n in range(8)],
    )
    proj_weight_grad = spread(
        place, feed_all, (2048, 1024), (32, 1024), 256, (2, 32),
        lambda a, g, place: (g, 2 + a, 0), lambda a, g, place: ((place[3] ^ a) * 32 + g, 0),
        [(0, n * 32, 32, 0, n * 128) for n in range(8)],
    )
    heads_full = in_order(core == 0, heads_all, heads_core).reshape(32, 576, 128)
    qkv_weight_grad = spread(
        place, heads_full, (512, 3072), (16, 3072), 576, (32,),
        lambda g, place: (g, 0, 0), lambda g, place: (g, 0),
        [
            (c, c * 112 + n * 16, 16, 256, (n // 2) * 1024 + (n % 2) * 128)
            for c in range(4)
            for n in range(6)
        ],
    )
    out_weight_grad = spread(
        place, heads_full, (512, 1024), (16, 512), 64, (2, 32),
        lambda a, g, place: (g, 7 + a, 0),
        lambda a, g, place: ((place[3] ^ a) * 16 + g % 16, g // 16),
        [(0, n * 16, 16, 0, n * 128) for n in range(4)],
    )

    return (
        hidden_out, hidden_grad, own_columns[1, 0], own_columns[1, 1], own_columns[0, 0],
        own_columns[0, 1], qkv_weight_grad, qkv_bias_grad, out_weight_grad, own_columns[0, 2],
        in_weight_grad, in_bias_grad, proj_weight_grad, own_columns[0, 2],
    )


def solution(mesh):
    fine = Mesh(mesh.devices.reshape(4, 4, 2, 2, 2), ("y", "z", "xl", "core", "xh"))
    ctx = ("y", "z", "xl", "core")
    rows = P("xh", ctx, None)
    half = P("xh")
    wide = P("xh", None)
    in_specs = (
        rows, wide, P(), half, half, half, half, wide, half, wide, half, wide, half, wide, half, rows,
    )
    out_specs = (
        rows, rows, half, half, half, half, wide, half, wide, half, wide, half, wide, half,
    )
    return jax.shard_map(
        per_device, mesh=fine, in_specs=in_specs, out_specs=out_specs, check_vma=False
    )
```

time: 543 us -> 421 us (0.78); the launches traced: 533 us -> 420 us
  waiting for transfers between devices: 215 us -> 113 us
  starting transfers between devices: 77.1 us -> 55.2 us
  local copies, waits for them, and re-layouts: 56.2 us -> 40.2 us
  between operations: 1.84 us -> 14.8 us
  blocking collectives: 14.7 us -> 27.2 us
  Pallas kernels: 118 us -> 130 us
  matrix products: 18.8 us -> 13 us
    all_to_all x6 -> x2, waiting for transfers between devices: 113 us -> 37.9 us  [to_all(): return lax.all_to_all(copies, axes, 0, 0, tiled=True)]
    pallas_call x2 -> x4, Pallas kernels: 22.8 us -> 66.6 us  [spread(): pl.pallas_call(functools.partial(spread_kernel, columns=columns), out_sha...]
    pallas_call x1, Pallas kernels: 83.2 us -> 45.6 us  [per_device(): call(attend_kernel, [shape(16, 320, 128)] * 2, [smem, smem] + [whole()] *...]
    ppermute x0 -> x12, waiting for transfers between devices: none -> 26 us  [shift_ring(): lax.ppermute(array_in, ('xl', 'xh'), [(spots[x], spots[(x + places) % 4])...]
    all_to_all x2 -> x1, waiting for transfers between devices: 25 us -> 0.01 us  [reduce_plane(): parts = lax.all_to_all(both, PLANE, 0, 0, tiled=True)]
    ppermute x0 -> x12, starting transfers between devices: none -> 20.9 us  [shift_ring(): lax.ppermute(array_in, ('xl', 'xh'), [(spots[x], spots[(x + places) % 4])...]
    all_to_all x6 -> x2, starting transfers between devices: 33.4 us -> 12.6 us  [to_all(): return lax.all_to_all(copies, axes, 0, 0, tiled=True)]
    all_to_all x4 -> x0, starting transfers between devices: 17.7 us -> none  [the longest x1 6.04 us: per_device(): grads_own = lax.all_to_all(grad_send, PLANE, 0, 0, tiled=True)]
  transfers between devices with their start and end apart: 27 -> 28, of which waited for: 16 -> 15; matrix products, arithmetic and copies ran while one was open for 13% -> 14% of each run, Pallas kernels for 4% -> 23%
where the time goes in v2:
time: 421 us; the launch traced here: 420 us
  Pallas kernels  130 us (31%)
  waiting for transfers between devices  113 us (27%)
  starting transfers between devices  55.2 us (13%)
  local copies, waits for them, and re-layouts  40.2 us (10%)
  blocking collectives  27.2 us (6%)
  other arithmetic  26.1 us (6%)
  between operations  14.8 us (4%)
  matrix products  13 us (3%)
    pallas_call x4, Pallas kernels, spread(): pl.pallas_call(functools.partial(spread_kernel, columns=columns), out_sha...  66.6 us
    pallas_call x1, Pallas kernels, per_device(): call(attend_kernel, [shape(16, 320, 128)] * 2, [smem, smem] + [whole()] *...  45.6 us
    all_to_all x2, waiting for transfers between devices, to_all(): return lax.all_to_all(copies, axes, 0, 0, tiled=True)  37.9 us
    all_to_all x1, blocking collectives, reduce_plane(): parts = lax.all_to_all(both, PLANE, 0, 0, tiled=True)  27.2 us
    all_to_all x1, waiting for transfers between devices, per_device(): lax.all_to_all(jnp.concatenate([back_own[:, :256] + arrived[:, :256], bac...  27.1 us
    ppermute x12, waiting for transfers between devices, shift_ring(): lax.ppermute(array_in, ('xl', 'xh'), [(spots[x], spots[(x + places) % 4])...  26 us
    ppermute x12, starting transfers between devices, shift_ring(): lax.ppermute(array_in, ('xl', 'xh'), [(spots[x], spots[(x + places) % 4])...  20.9 us
    unnamed x84, local copies, waits for them, and re-layouts  17.3 us
  transfers between devices with their start and end apart: 28, of which 15 were waited for; matrix products, arithmetic and copies ran while one was open for 14% of the time, Pallas kernels for 23%

profile of v2, /device:TPU:0, one launch (start us, length us, event | category | flops | bytes accessed | tf_op | source)
XLA Modules:
  0.0 419.5 jit_solution(9577332458858362752)
XLA Ops:
  9.2 1.6 collective-permute-start
  10.9 2.7 collective-permute-start.1
  15.0 1.5 fusion.36
  18.0 5.6 %concatenate.96 = bf16[7168]{0:T(1024)(128)(2,1)S(1)} concatenate(bf16[512]{0:T(512)(128)(2,1)} %param.19, bf16[512]{0:T(512)(128)(2,1)} %param.20, bf16[512]{0:T(512)(128)(2,1)} %param.21, bf16[512]{0:T(512)(128)(2,1)} %param.22, bf16[1536]{0:T(1024)(128)(2,1)} %param.24, bf16[2048]{0:T(1024)(128)(2,1)} %param.28, bf16[512]{0:T(512)(128)(2,1)} %param.26, bf16[512]{0:T(512)(128)(2,1)} %param.30, ...), dimensions={0} | concatenate | bytes 28672 | tf_op jit(solution)/shard_map/concatenate | solution.py:439
  25.4 3.1 collective-permute-start.4
  30.2 2.3 dynamic-slice_bitcast_fusion
  40.1 8.0 %all-to-all-start = ((bf16[16,32,768]{2,1,0:T(8,128)(2,1)}), bf16[16,32,768]{2,1,0:T(8,128)(2,1)S(1)}, u32[]{:S(2)}, u32[]{:S(2)}) async-start(bf16[16,32,768]{2,1,0:T(8,128)(2,1)} %broadcast_in_dim.66), calls=%async_computation | async-start | bytes 1572864 | tf_op jit(solution)/shard_map/all_to_all | solution.py:52
  48.4 2.9 collective-permute-done.6
  52.4 8.4 %all-to-all-done = bf16[16,32,768]{2,1,0:T(8,128)(2,1)S(1)} async-done(((bf16[16,32,768]{2,1,0:T(8,128)(2,1)}), bf16[16,32,768]{2,1,0:T(8,128)(2,1)S(1)}, u32[]{:S(2)}, u32[]{:S(2)}) %all-to-all-start) | async-done | bytes 786464 | tf_op jit(solution)/shard_map/all_to_all | solution.py:52
  60.8 6.0 %shard_map.263 = (bf16[16,384,128]{2,1,0:T(8,128)(2,1)}, bf16[512,1024]{1,0:T(8,128)(2,1)S(1)}, bf16[512,1024]{1,0:T(8,128)(2,1)}, bf16[512,1024]{1,0:T(8,128)(2,1)}, bf16[512,1024]{1,0:T(8,128)(2,1)}) custom-call(s32[4]{0:T(128)S(1)} %pad_add_fusion.place, bf16[2,128,1024]{2,1,0:T(8,128)(2,1)S(1)} %constant_dynamic-update-slice_fusion.rows0, ...), custom_call_target="tpu_custom_call" | custom-call | flops 1073741824 | bytes 12582912 | tf_op jit(solution)/shard_map/pallas_call | solution.py:473
  67.8 3.9 all-to-all-start.1
  71.7 1.8 maximum_select_fusion.3
  77.5 2.1 convert_reduce_fusion
  79.6 4.6 %shard_map.264 = (bf16[16,512,128]{2,1,0:T(8,128)(2,1)}, bf16[16,512,128]{2,1,0:T(8,128)(2,1)}) custom-call(s32[4]{0:T(128)S(1)} %pad_add_fusion.place, bf16[512,1024]{1,0:T(8,128)(2,1)S(1)} %copy-done.14, bf16[512,1024]{1,0:T(8,128)(2,1)S(1)} %get-tuple-element.111.inner_grad, bf16[512,1024]{1,0:T(8,128)(2,1)S(1)} %get-tuple-element.108.active, ...), custom_call_target="tpu_custom_call" | custom-call | flops 2147483648 | bytes 8388608 | tf_op jit(solution)/shard_map/pallas_call | solution.py:508
  84.2 8.7 %all-to-all-done.1.own = bf16[16,384,128]{2,1,0:T(8,128)(2,1)S(1)} async-done(((bf16[16,384,128]{2,1,0:T(8,128)(2,1)}), bf16[16,384,128]{2,1,0:T(8,128)(2,1)S(1)}, u32[]{:S(2)}, u32[]{:S(2)}) %all-to-all-start.1) | async-done | bytes 1572896 | tf_op jit(solution)/shard_map/all_to_all | solution.py:481
  93.1 5.0 %multiply_reduce_fusion = (f32[1024]{0:T(1024)S(1)}, f32[1024]{0:T(1024)S(1)}, f32[512,1024]{1,0:T(8,128)}) fusion(bf16[512,1024]{1,0:T(8,128)(2,1)} %get-tuple-element.39.xhat, f32[1024]{0:T(1024)S(1)} %bitcast.222, bf16[512,1024]{1,0:T(8,128)(2,1)} %copy-done.17, bf16[1024,1024]{1,0:T(8,128)(2,1)} %bitcast.201), kind=kOutput, calls=%fused_computation.21 | convolution fusion | flops 1076361216 | bytes 6303744 | tf_op jit(solution)/shard_map/dot_general | solution.py:27
  98.2 2.6 fusion.6
  100.7 3.7 add.488
  104.4 4.6 %all-to-all-start.5 = ((bf16[16,512,128]{2,1,0:T(8,128)(2,1)}), bf16[16,512,128]{2,1,0:T(8,128)(2,1)}, u32[]{:S(2)}, u32[]{:S(2)}) async-start(bf16[16,512,128]{2,1,0:T(8,128)(2,1)} %add.488), calls=%async_computation.5 | async-start | bytes 4194304 | tf_op jit(solution)/shard_map/all_to_all | solution.py:518
  109.1 45.6 %shard_map.265 = (bf16[16,320,128]{2,1,0:T(8,128)(2,1)S(1)}, bf16[16,320,128]{2,1,0:T(8,128)(2,1)S(1)}) custom-call(s32[4]{0:T(128)S(1)} %pad_add_fusion.2.place, s32[64]{0:T(128)S(1)} %copy-done.2, bf16[16,384,128]{2,1,0:T(8,128)(2,1)S(1)} %all-to-all-done.1.own, bf16[16,384,128]{2,1,0:T(8,128)(2,1)} %collective-permute-done.5.other), custom_call_target="tpu_custom_call" | custom-call | flops 44999999488 | bytes 6291456 | tf_op jit(solution)/shard_map/pallas_call | solution.py:537
  156.8 2.0 reduce_sum.138
  159.9 3.1 collective-permute-start.19
  163.0 1.8 collective-permute-start.20
  169.5 2.9 collective-permute-done.21
  173.2 3.2 collective-permute-done.9
  177.8 7.3 %all-to-all-start.2 = ((bf16[16,384,128]{2,1,0:T(8,128)(2,1)}), bf16[16,384,128]{2,1,0:T(8,128)(2,1)}, u32[]{:S(2)}, u32[]{:S(2)}) async-start(bf16[16,384,128]{2,1,0:T(8,128)(2,1)} %pad_maximum_fusion), calls=%async_computation.2 | async-start | bytes 3145728 | tf_op jit(solution)/shard_map/all_to_all | solution.py:555
  186.5 27.1 %all-to-all-done.2.back = bf16[16,384,128]{2,1,0:T(8,128)(2,1)} async-done(((bf16[16,384,128]{2,1,0:T(8,128)(2,1)}), bf16[16,384,128]{2,1,0:T(8,128)(2,1)}, u32[]{:S(2)}, u32[]{:S(2)}) %all-to-all-start.2) | async-done | bytes 1572896 | tf_op jit(solution)/shard_map/all_to_all | solution.py:555
  217.3 7.0 %shard_map.266 = (bf16[16,272,128]{2,1,0:T(8,128)(2,1)S(1)}, bf16[16,272,128]{2,1,0:T(8,128)(2,1)}, f32[512,1024]{1,0:T(8,128)}, bf16[512,768]{1,0:T(8,128)(2,1)}, bf16[512,256]{1,0:T(8,128)(2,1)S(1)}) custom-call(s32[4]{0:T(128)S(1)} %pad_add_fusion.place, bf16[16,384,128]{2,1,0:T(8,128)(2,1)} %all-to-all-done.2.back, f32[512,128]{1,0:T(8,128)S(1)} %copy-done.7, ...), custom_call_target="tpu_custom_call" | custom-call | flops 2147483648 | bytes 9437184 | tf_op jit(solution)/shard_map/pallas_call | solution.py:569
  224.3 3.0 collective-permute-done.13
  227.6 27.2 %all_to_all.30 = bf16[16,272,128]{2,1,0:T(8,128)(2,1)S(1)} all-to-all(bf16[16,272,128]{2,1,0:T(8,128)(2,1)S(1)} %add.506), channel_id=1, replica_groups=mesh['y'=4,'z'=4,'xl'=2,'core'=2,'xh'=2] {'y','z'}, dimensions={0} | all-to-all | bytes 2228224 | tf_op jit(solution)/shard_map/all_to_all | solution.py:518
  255.0 1.5 collective-permute-start.14
  256.6 2.7 collective-permute-start.15
  259.2 1.5 collective-permute-start.16
  263.3 1.9 broadcast_in_dim.72
  265.2 4.6 %all-to-all-start.4 = ((bf16[16,576,128]{2,1,0:T(8,128)(2,1)}), bf16[16,576,128]{2,1,0:T(8,128)(2,1)}, u32[]{:S(2)}, u32[]{:S(2)}) async-start(bf16[16,576,128]{2,1,0:T(8,128)(2,1)} %broadcast_in_dim.72), calls=%async_computation.4 | async-start | bytes 4718592 | tf_op jit(solution)/shard_map/all_to_all | solution.py:52
  270.2 1.9 fusion.63
  272.0 29.5 %all-to-all-done.4 = bf16[16,576,128]{2,1,0:T(8,128)(2,1)} async-done(((bf16[16,576,128]{2,1,0:T(8,128)(2,1)}), bf16[16,576,128]{2,1,0:T(8,128)(2,1)}, u32[]{:S(2)}, u32[]{:S(2)}) %all-to-all-start.4) | async-done | bytes 2359328 | tf_op jit(solution)/shard_map/all_to_all | solution.py:52
  301.5 2.7 add_convert_fusion.1
  305.7 3.9 collective-permute-start.11
  309.7 11.3 %collective-permute-done.12 = bf16[256,1024]{1,0:T(8,128)(2,1)S(1)} collective-permute-done((bf16[256,1024]{1,0:T(8,128)(2,1)S(1)}, bf16[256,1024]{1,0:T(8,128)(2,1)S(1)}, u32[]{:S(2)}, u32[]{:S(2)}) %collective-permute-start.12) | collective-permute-done | bytes 524320 | tf_op jit(solution)/shard_map/ppermute | solution.py:61
  321.0 11.3 %collective-permute-done.11 = bf16[256,1024]{1,0:T(8,128)(2,1)S(1)} collective-permute-done((bf16[256,1024]{1,0:T(8,128)(2,1)S(1)}, bf16[256,1024]{1,0:T(8,128)(2,1)S(1)}, u32[]{:S(2)}, u32[]{:S(2)}) %collective-permute-start.11) | collective-permute-done | bytes 524320 | tf_op jit(solution)/shard_map/ppermute | solution.py:61
  334.0 1.6 slice.207
  335.6 3.3 maximum_select_fusion
  338.9 11.8 %shard_map.267 = f32[512,3072]{1,0:T(8,128)} custom-call(s32[4]{0:T(128)S(1)} %pad_add_fusion.place, bf16[32,576,128]{2,1,0:T(8,128)(2,1)S(1)} %bitcast.181), custom_call_target="tpu_custom_call" | custom-call | bytes 9437184 | tf_op jit(solution)/shard_map/pallas_call | solution.py:377
  350.7 20.4 %shard_map.268 = f32[512,1024]{1,0:T(8,128)} custom-call(s32[4]{0:T(128)S(1)} %pad_add_fusion.place, bf16[32,576,128]{2,1,0:T(8,128)(2,1)S(1)} %bitcast.182), custom_call_target="tpu_custom_call" | custom-call | bytes 3145728 | tf_op jit(solution)/shard_map/pallas_call | solution.py:377
  374.3 3.4 copy-done.3
  377.7 12.5 %shard_map.269 = f32[512,4096]{1,0:T(8,128)} custom-call(s32[4]{0:T(128)S(1)} %pad_add_fusion.place, bf16[32,1024,128]{2,1,0:T(8,128)(2,1)S(1)} %bitcast.183), custom_call_target="tpu_custom_call" | custom-call | bytes 12582912 | tf_op jit(solution)/shard_map/pallas_call | solution.py:377
  390.3 21.8 %shard_map.270 = f32[2048,1024]{1,0:T(8,128)} custom-call(s32[4]{0:T(128)S(1)} %pad_add_fusion.place, bf16[32,1024,128]{2,1,0:T(8,128)(2,1)S(1)} %bitcast.184), custom_call_target="tpu_custom_call" | custom-call | bytes 12582912 | tf_op jit(solution)/shard_map/pallas_call | solution.py:377
  (204 shorter events, 47.9 us)
Async XLA Ops:
  7.2 22.9 %copy-start = (bf16[512,1024]{1,0:T(8,128)(2,1)S(1)}, bf16[512,1024]{1,0:T(8,128)(2,1)}, u32[]{:S(2)}) copy-start(bf16[512,1024]{1,0:T(8,128)(2,1)} %param.25) | copy-start | bytes 3145732
  9.2 43.1 %collective-permute-start = (bf16[2,128,1024]{2,1,0:T(8,128)(2,1)S(1)}, bf16[2,128,1024]{2,1,0:T(8,128)(2,1)}, u32[]{:S(2)}, u32[]{:S(2)}) collective-permute-start(bf16[2,128,1024]{2,1,0:T(8,128)(2,1)S(1)} %constant_dynamic-update-slice_fusion.rows0), channel_id=1, source_target_pairs={{0,4},{4,1},{1,5},{5,0},{2,6},{6,3},{3,7},{7,2},{8,12},{12,9},{9,1... | collective-permute-start | bytes 1572872 | tf_op jit(solution)/shard_map/ppermute | solution.py:61
  10.9 41.5 %collective-permute-start.1 = (bf16[2,128,1024]{2,1,0:T(8,128)(2,1)S(1)}, bf16[2,128,1024]{2,1,0:T(8,128)(2,1)}, u32[]{:S(2)}, u32[]{:S(2)}) collective-permute-start(bf16[2,128,1024]{2,1,0:T(8,128)(2,1)S(1)} %constant_dynamic-update-slice_fusion.rows0), channel_id=1, source_target_pairs={{0,1},{4,5},{1,0},{5,4},{2,3},{6,7},{3,2},{7,6},{8,9},{12,13},{9,8... | collective-permute-start | bytes 1572872 | tf_op jit(solution)/shard_map/ppermute | solution.py:61
  13.6 38.8 %collective-permute-start.2 = (bf16[2,128,1024]{2,1,0:T(8,128)(2,1)S(1)}, bf16[2,128,1024]{2,1,0:T(8,128)(2,1)}, u32[]{:S(2)}, u32[]{:S(2)}) collective-permute-start(bf16[2,128,1024]{2,1,0:T(8,128)(2,1)S(1)} %constant_dynamic-update-slice_fusion.rows0), channel_id=1, source_target_pairs={{0,5},{4,0},{1,4},{5,1},{2,7},{6,2},{3,6},{7,3},{8,13},{12,8},{9,1... | collective-permute-start | bytes 1572872 | tf_op jit(solution)/shard_map/ppermute | solution.py:61
  23.6 13.7 %collective-permute-start.3 = (bf16[56,128]{1,0:T(8,128)(2,1)S(1)}, bf16[56,128]{1,0:T(8,128)(2,1)S(1)}, u32[]{:S(2)}, u32[]{:S(2)}) collective-permute-start(bf16[56,128]{1,0:T(8,128)(2,1)S(1)} %bitcast.209), channel_id=1, source_target_pairs={{0,1},{1,0},{2,3},{3,2},{4,5},{5,4},{6,7},{7,6},{8,9},{9,8},{10,11... | collective-permute-start | bytes 43016 | tf_op jit(solution)/shard_map/ppermute | solution.py:56
  25.4 13.7 %collective-permute-start.4 = (bf16[32,768]{1,0:T(8,128)(2,1)}, bf16[32,768]{1,0:T(8,128)(2,1)S(1)}, u32[]{:S(2)}, u32[]{:S(2)}) collective-permute-start(bf16[32,768]{1,0:T(8,128)(2,1)} %pad_maximum_fusion.11), channel_id=1, source_target_pairs={{0,1},{1,0},{2,3},{3,2},{4,5},{5,4},{6,7},{7,6},{8,9},{9,8},{10,11... | collective-permute-start | bytes 147464 | tf_op jit(solution)/shard_map/ppermute | solution.py:56
  37.3 14.0 %collective-permute-start.6 = (bf16[256,1024]{1,0:T(8,128)(2,1)S(1)}, bf16[256,1024]{1,0:T(8,128)(2,1)}, u32[]{:S(2)}, u32[]{:S(2)}) collective-permute-start(bf16[256,1024]{1,0:T(8,128)(2,1)S(1)} %dynamic_slice.85), channel_id=1, source_target_pairs={{0,1},{1,0},{2,3},{3,2},{4,5},{5,4},{6,7},{7,6},{8,9},{9,8},{10,11... | collective-permute-start | bytes 1572872 | tf_op jit(solution)/shard_map/ppermute | solution.py:56
  40.1 20.8 %all-to-all-start = ((bf16[16,32,768]{2,1,0:T(8,128)(2,1)}), bf16[16,32,768]{2,1,0:T(8,128)(2,1)S(1)}, u32[]{:S(2)}, u32[]{:S(2)}) async-start(bf16[16,32,768]{2,1,0:T(8,128)(2,1)} %broadcast_in_dim.66), calls=%async_computation | async-start | bytes 1572864 | tf_op jit(solution)/shard_map/all_to_all | solution.py:52
  51.3 20.4 %collective-permute-start.7 = (bf16[256,1024]{1,0:T(8,128)(2,1)}, bf16[256,1024]{1,0:T(8,128)(2,1)}, u32[]{:S(2)}, u32[]{:S(2)}) collective-permute-start(bf16[256,1024]{1,0:T(8,128)(2,1)} %collective-permute-done.6), channel_id=1, source_target_pairs={{0,2},{2,0},{1,3},{3,1},{4,6},{6,4},{5,7},{7,5},{8,10},{10,8},{9,1... | collective-permute-start | bytes 1572872 | tf_op jit(solution)/shard_map/ppermute | solution.py:56
  52.4 14.5 %copy-start.6 = (f32[512,128]{1,0:T(8,128)}, f32[512,128]{1,0:T(8,128)S(1)}, u32[]{:S(2)}) copy-start(f32[512,128]{1,0:T(8,128)S(1)} %get-tuple-element.107.cosine) | copy-start | bytes 786436
  67.8 25.1 %all-to-all-start.1 = ((bf16[16,384,128]{2,1,0:T(8,128)(2,1)}), bf16[16,384,128]{2,1,0:T(8,128)(2,1)S(1)}, u32[]{:S(2)}, u32[]{:S(2)}) async-start(bf16[16,384,128]{2,1,0:T(8,128)(2,1)} %get-tuple-element.34), calls=%async_computation.1 | async-start | bytes 3145728 | tf_op jit(solution)/shard_map/all_to_all | solution.py:481
  73.9 2.3 copy-start.24
  74.8 2.7 copy-start.27
  76.3 3.3 copy-start.15
  79.6 4.7 %copy-start.17 = (bf16[512,1024]{1,0:T(8,128)(2,1)}, bf16[512,1024]{1,0:T(8,128)(2,1)S(1)}, u32[]{:S(2)}) copy-start(bf16[512,1024]{1,0:T(8,128)(2,1)S(1)} %get-tuple-element.111.inner_grad) | copy-start | bytes 3145732
  79.6 13.3 %copy-start.21 = (bf16[1,128,1024]{2,1,0:T(8,128)(2,1)S(1)}, bf16[1,128,1024]{2,1,0:T(8,128)(2,1)}, u32[]{:S(2)}) copy-start(bf16[1,128,1024]{2,1,0:T(8,128)(2,1)} %param.31) | copy-start | bytes 786436
  84.2 16.5 %collective-permute-start.8 = (bf16[16,512,128]{2,1,0:T(8,128)(2,1)}, bf16[16,512,128]{2,1,0:T(8,128)(2,1)}, u32[]{:S(2)}, u32[]{:S(2)}) collective-permute-start(bf16[16,512,128]{2,1,0:T(8,128)(2,1)} %get-tuple-element.38), channel_id=1, source_target_pairs={{0,2},{2,0},{1,3},{3,1},{4,6},{6,4},{5,7},{7,5},{8,10},{10,8},{9,1... | collective-permute-start | bytes 6291464 | tf_op jit(solution)/shard_map/ppermute | solution.py:56
  92.9 11.5 %collective-permute-start.5 = (bf16[16,384,128]{2,1,0:T(8,128)(2,1)S(1)}, bf16[16,384,128]{2,1,0:T(8,128)(2,1)}, u32[]{:S(2)}, u32[]{:S(2)}) collective-permute-start(bf16[16,384,128]{2,1,0:T(8,128)(2,1)S(1)} %all-to-all-done.1.own), channel_id=1, source_target_pairs={{0,2},{2,0},{1,3},{3,1},{4,6},{6,4},{5,7},{7,5},{8,10},{10,8},{9,1... | collective-permute-start | bytes 4718600 | tf_op jit(solution)/shard_map/ppermute | solution.py:56
  93.1 5.0 %copy-start.16 = (bf16[512,1024]{1,0:T(8,128)(2,1)S(1)}, bf16[512,1024]{1,0:T(8,128)(2,1)}, u32[]{:S(2)}) copy-start(bf16[512,1024]{1,0:T(8,128)(2,1)} %copy-done.15) | copy-start | bytes 3145732
  93.1 5.0 %copy-start.28 = (bf16[2048,1024]{1,0:T(8,128)(2,1)S(1)}, bf16[2048,1024]{1,0:T(8,128)(2,1)}, u32[]{:S(2)}) copy-start(bf16[2048,1024]{1,0:T(8,128)(2,1)} %param.29) | copy-start | bytes 12582916
  98.1 2.6 copy-start.22
  104.4 4.6 %copy-start.2 = (s32[64]{0:T(128)S(1)}, s32[64]{0:T(128)}, u32[]{:S(2)}) copy-start(s32[64]{0:T(128)} %block_map.1) | copy-start | bytes 772
  104.4 52.4 %all-to-all-start.5 = ((bf16[16,512,128]{2,1,0:T(8,128)(2,1)}), bf16[16,512,128]{2,1,0:T(8,128)(2,1)}, u32[]{:S(2)}, u32[]{:S(2)}) async-start(bf16[16,512,128]{2,1,0:T(8,128)(2,1)} %add.488), calls=%async_computation.5 | async-start | bytes 4194304 | tf_op jit(solution)/shard_map/all_to_all | solution.py:518
  109.0 265.3 %all-gather.3.cloned.1.call-start = ((), (), s32[]{:S(2)}) async-start(), calls=%async_computation.6 | async-start | bytes 8650752 | tf_op jit(solution)/shard_map/all_gather | solution.py:564
  156.8 16.4 %copy-start.5 = (bf16[16,320,128]{2,1,0:T(8,128)(2,1)S(1)}, bf16[16,320,128]{2,1,0:T(8,128)(2,1)}, u32[]{:S(2)}) copy-start(bf16[16,320,128]{2,1,0:T(8,128)(2,1)} %copy-done.4) | copy-start | bytes 3932164
  158.8 6.0 %collective-permute-start.18 = (bf16[128,128]{1,0:T(8,128)(2,1)S(1)}, bf16[128,128]{1,0:T(8,128)(2,1)S(1)}, u32[]{:S(2)}, u32[]{:S(2)}) collective-permute-start(bf16[128,128]{1,0:T(8,128)(2,1)S(1)} %get-tuple-element.88), channel_id=1, source_target_pairs={{0,4},{4,1},{1,5},{5,0},{2,6},{6,3},{3,7},{7,2},{8,12},{12,9},{9,1... | collective-permute-start | bytes 98312 | tf_op jit(solution)/shard_map/ppermute | solution.py:61
  159.9 5.5 %collective-permute-start.19 = (bf16[128,128]{1,0:T(8,128)(2,1)S(1)}, bf16[128,128]{1,0:T(8,128)(2,1)S(1)}, u32[]{:S(2)}, u32[]{:S(2)}) collective-permute-start(bf16[128,128]{1,0:T(8,128)(2,1)S(1)} %get-tuple-element.87), channel_id=1, source_target_pairs={{0,1},{4,5},{1,0},{5,4},{2,3},{6,7},{3,2},{7,6},{8,9},{12,13},{9,8... | collective-permute-start | bytes 98312 | tf_op jit(solution)/shard_map/ppermute | solution.py:61
  163.0 3.9 collective-permute-start.20
  168.2 4.3 %collective-permute-start.21 = (bf16[256,128]{1,0:T(8,128)(2,1)S(1)}, bf16[256,128]{1,0:T(8,128)(2,1)S(1)}, u32[]{:S(2)}, u32[]{:S(2)}) collective-permute-start(bf16[256,128]{1,0:T(8,128)(2,1)S(1)} %get-tuple-element.82), channel_id=1, source_target_pairs={{0,4},{4,0},{1,5},{5,1},{2,6},{6,2},{3,7},{7,3},{8,12},{12,8},{9,1... | collective-permute-start | bytes 196616 | tf_op jit(solution)/shard_map/ppermute | solution.py:56
  173.1 3.3 collective-permute-start.9
  177.8 7.3 %copy-start.20 = (bf16[1,512,768]{2,1,0:T(8,128)(2,1)S(1)}, bf16[1,512,768]{2,1,0:T(8,128)(2,1)}, u32[]{:S(2)}) copy-start(bf16[1,512,768]{2,1,0:T(8,128)(2,1)} %get-tuple-element.80) | copy-start | bytes 2359300
  177.8 35.8 %all-to-all-start.2 = ((bf16[16,384,128]{2,1,0:T(8,128)(2,1)}), bf16[16,384,128]{2,1,0:T(8,128)(2,1)}, u32[]{:S(2)}, u32[]{:S(2)}) async-start(bf16[16,384,128]{2,1,0:T(8,128)(2,1)} %pad_maximum_fusion), calls=%async_computation.2 | async-start | bytes 3145728 | tf_op jit(solution)/shard_map/all_to_all | solution.py:555
  185.1 28.6 %copy-start.7 = (f32[512,128]{1,0:T(8,128)S(1)}, f32[512,128]{1,0:T(8,128)}, u32[]{:S(2)}) copy-start(f32[512,128]{1,0:T(8,128)} %copy-done.6) | copy-start | bytes 786436
  224.3 3.0 collective-permute-start.13
  255.0 5.8 %collective-permute-start.14 = (bf16[176,128]{1,0:T(8,128)(2,1)S(1)}, bf16[176,128]{1,0:T(8,128)(2,1)S(1)}, u32[]{:S(2)}, u32[]{:S(2)}) collective-permute-start(bf16[176,128]{1,0:T(8,128)(2,1)S(1)} %get-tuple-element.105), channel_id=1, source_target_pairs={{0,4},{4,1},{1,5},{5,0},{2,6},{6,3},{3,7},{7,2},{8,12},{12,9},{9,1... | collective-permute-start | bytes 135176 | tf_op jit(solution)/shard_map/ppermute | solution.py:61
  256.6 5.6 %collective-permute-start.15 = (bf16[176,128]{1,0:T(8,128)(2,1)S(1)}, bf16[176,128]{1,0:T(8,128)(2,1)S(1)}, u32[]{:S(2)}, u32[]{:S(2)}) collective-permute-start(bf16[176,128]{1,0:T(8,128)(2,1)S(1)} %get-tuple-element.104), channel_id=1, source_target_pairs={{0,1},{4,5},{1,0},{5,4},{2,3},{6,7},{3,2},{7,6},{8,9},{12,13},{9,8... | collective-permute-start | bytes 135176 | tf_op jit(solution)/shard_map/ppermute | solution.py:61
  259.2 4.0 collective-permute-start.16
  265.2 4.6 %copy-start.18 = (bf16[1,128,1024]{2,1,0:T(8,128)(2,1)S(1)}, bf16[1,128,1024]{2,1,0:T(8,128)(2,1)}, u32[]{:S(2)}) copy-start(bf16[1,128,1024]{2,1,0:T(8,128)(2,1)} %param.16) | copy-start | bytes 786436
  265.2 36.3 %all-to-all-start.4 = ((bf16[16,576,128]{2,1,0:T(8,128)(2,1)}), bf16[16,576,128]{2,1,0:T(8,128)(2,1)}, u32[]{:S(2)}, u32[]{:S(2)}) async-start(bf16[16,576,128]{2,1,0:T(8,128)(2,1)} %broadcast_in_dim.72), calls=%async_computation.4 | async-start | bytes 4718592 | tf_op jit(solution)/shard_map/all_to_all | solution.py:52
  301.5 2.9 copy-start.23
  301.5 3.5 copy-start.25
  301.5 34.1 %collective-permute-start.17 = (bf16[16,576,128]{2,1,0:T(8,128)(2,1)}, bf16[16,576,128]{2,1,0:T(8,128)(2,1)S(1)}, u32[]{:S(2)}, u32[]{:S(2)}) collective-permute-start(bf16[16,576,128]{2,1,0:T(8,128)(2,1)} %all-to-all-done.4), channel_id=1, source_target_pairs={{0,2},{2,0},{1,3},{3,1},{4,6},{6,4},{5,7},{7,5},{8,10},{10,8},{9,1... | collective-permute-start | bytes 7077896 | tf_op jit(solution)/shard_map/ppermute | solution.py:56
  305.6 15.4 %collective-permute-start.12 = (bf16[256,1024]{1,0:T(8,128)(2,1)S(1)}, bf16[256,1024]{1,0:T(8,128)(2,1)S(1)}, u32[]{:S(2)}, u32[]{:S(2)}) collective-permute-start(bf16[256,1024]{1,0:T(8,128)(2,1)S(1)} %get-tuple-element.75), channel_id=1, source_target_pairs={{0,4},{4,1},{1,5},{5,0},{2,6},{6,3},{3,7},{7,2},{8,12},{12,9},{9,1... | collective-permute-start | bytes 1572872 | tf_op jit(solution)/shard_map/ppermute | solution.py:61
  305.7 26.5 %collective-permute-start.11 = (bf16[256,1024]{1,0:T(8,128)(2,1)S(1)}, bf16[256,1024]{1,0:T(8,128)(2,1)S(1)}, u32[]{:S(2)}, u32[]{:S(2)}) collective-permute-start(bf16[256,1024]{1,0:T(8,128)(2,1)S(1)} %get-tuple-element.76), channel_id=1, source_target_pairs={{0,1},{4,5},{1,0},{5,4},{2,3},{6,7},{3,2},{7,6},{8,9},{12,13},{9,8... | collective-permute-start | bytes 1572872 | tf_op jit(solution)/shard_map/ppermute | solution.py:61
  309.7 22.6 %collective-permute-start.10 = (bf16[256,1024]{1,0:T(8,128)(2,1)S(1)}, bf16[256,1024]{1,0:T(8,128)(2,1)S(1)}, u32[]{:S(2)}, u32[]{:S(2)}) collective-permute-start(bf16[256,1024]{1,0:T(8,128)(2,1)S(1)} %get-tuple-element.74), channel_id=1, source_target_pairs={{0,5},{4,0},{1,4},{5,1},{2,7},{6,2},{3,6},{7,3},{8,13},{12,8},{9,1... | collective-permute-start | bytes 1572872 | tf_op jit(solution)/shard_map/ppermute | solution.py:61
  373.1 39.1 %copy-start.26 = (f32[1,1,512]{2,1,0:T(1,128)}, f32[1,1,512]{2,1,0:T(1,128)S(1)}, u32[]{:S(2)}) copy-start(f32[1,1,512]{2,1,0:T(1,128)S(1)} %get-tuple-element.92) | copy-start | bytes 6148
  374.3 3.4 copy-start.3
  390.3 22.4 %copy-start.1 = (bf16[512,1024]{1,0:T(8,128)(2,1)S(1)}, bf16[512,1024]{1,0:T(8,128)(2,1)}, u32[]{:S(2)}) copy-start(bf16[512,1024]{1,0:T(8,128)(2,1)} %param.25) | copy-start | bytes 3145732
  (9 other events, 11.3 us)
Sparse Core Ops, SparseCore 0:
  173.2 78.7 all-gather.2
